TPU v7x, 512 devices: a whole 4x8x8 slice. The times are simulated.
512 devices in a mesh: seq: 16 (over z, core), exp: 32 (over y, x).
Axes of the slice: x: 4, y: 8, z: 8, core: 2. Of those that a mesh axis runs over, the one named last changes fastest.
Arguments:
- query_rows: bfloat16 [32768, 1024], P(('exp', 'seq')), may hold values from -8 to 8
- key_rows: bfloat16 [32768, 1024], P(('exp', 'seq')), may hold values from -8 to 8
- value_rows: bfloat16 [32768, 1024], P(('exp', 'seq')), may hold values from -6 to 6
- query_tangent: bfloat16 [32768, 1024], P(('exp', 'seq')), may hold values from -6 to 6
- key_tangent: bfloat16 [32768, 1024], P(('exp', 'seq')), may hold values from -6 to 6
- value_tangent: bfloat16 [32768, 1024], P(('exp', 'seq')), may hold values from -6 to 6
- stream: bfloat16 [32768, 1024], P(('exp', 'seq')), may hold values from -16 to 16
- stream_tangent: bfloat16 [32768, 1024], P(('exp', 'seq')), may hold values from -6 to 6
- norm_gain: float32 [1024], replicated, may hold values from 0.1 to 1.9
- expert_ids: int32 [32768, 2], P(('exp', 'seq')), may hold values from 0 to 15, as said below
- gate_units: int32 [32768, 2], P(('exp', 'seq')), may hold values from 4096 to 61440, as said below
- slot_index: int32 [32768, 2], P(('exp', 'seq')), may hold values from -1 to 9, as said below
- weight_in: bfloat16 [1024, 65536], P(None, ('exp', 'seq')), may hold values from -0.1875 to 0.1875
- weight_out: bfloat16 [65536, 1024], P(('exp', 'seq')), may hold values from -0.09375 to 0.09375
Outputs:
- block_out: bfloat16 [32768, 1024], P(('exp', 'seq'))
- block_tangent: bfloat16 [32768, 1024], P(('exp', 'seq'))
Inputs may be any that keep to these rules, and one draw needn't show every extreme that they name: `expert_ids`: each token names two different experts. In every aligned block of 64 rows one expert is named by more than 10 tokens. `gate_units`: the two gates of a token sum to 65536; the first is the larger or equal one. `slot_index`: within an aligned block of 64 rows the kept assignments to one expert hold the slots 0, 1, 2 and so on, each once, in no particular order; assignments beyond 10 are -1. Every block fills all 10 slots of some expert.
All inputs are finite; a program needn't handle non-finite values.
Results may differ from a plain program's by a relative error of at most 0.0059.
Values may be sent and summed in bfloat16 or wider, within the bound.
A program may use at most 64 MiB of HBM per device.

v0:
```python
import jax
import jax.numpy as jnp
from jax import lax
from jax.sharding import PartitionSpec as P

HEAD_DIM = 64


epsilon = 1e-06
gelu_coef = 0.7978845608028654
cubic_coef = 0.044715


def gelu_pair(inputs, tangent):
    inner_arg = gelu_coef * (inputs + cubic_coef * inputs * inputs * inputs)
    hyperbolic = jnp.tanh(inner_arg)
    values = 0.5 * inputs * (1.0 + hyperbolic)
    slopes = 0.5 * (1.0 + hyperbolic) + 0.5 * inputs * (
        1.0 - hyperbolic * hyperbolic
    ) * gelu_coef * (1.0 + 3.0 * cubic_coef * inputs * inputs)
    return (values, slopes * tangent)


def per_device(
    query_rows,
    key_rows,
    value_rows,
    query_tangent,
    key_tangent,
    value_tangent,
    stream,
    stream_tangent,
    norm_gain,
    expert_ids,
    gate_units,
    slot_index,
    weight_in,
    weight_out,
):
    seq_count = lax.axis_size("seq")
    exp_count = lax.axis_size("exp")
    local_rows = stream.shape[0]
    model_width = stream.shape[1]
    group_rows = local_rows * seq_count
    expert_count = exp_count // 2
    capacity = 2 * ((5 * local_rows + 4 * expert_count - 1) // (4 * expert_count))
    heads_local = model_width // seq_count // HEAD_DIM
    score_scale = HEAD_DIM ** (-0.5)
    regrouped = (
        lax.all_to_all(query_rows, "seq", split_axis=1, concat_axis=0, tiled=True),
        lax.all_to_all(key_rows, "seq", split_axis=1, concat_axis=0, tiled=True),
        lax.all_to_all(value_rows, "seq", split_axis=1, concat_axis=0, tiled=True),
        lax.all_to_all(query_tangent, "seq", split_axis=1, concat_axis=0, tiled=True),
        lax.all_to_all(key_tangent, "seq", split_axis=1, concat_axis=0, tiled=True),
        lax.all_to_all(value_tangent, "seq", split_axis=1, concat_axis=0, tiled=True),
    )

    def by_heads(matrix):
        return matrix.reshape(group_rows, heads_local, HEAD_DIM)

    query_heads = by_heads(regrouped[0])
    keys_heads = by_heads(regrouped[1])
    values_heads = by_heads(regrouped[2])
    query_drift = by_heads(regrouped[3])
    keys_drift = by_heads(regrouped[4])
    values_drift = by_heads(regrouped[5])
    scores = (
        jnp.einsum("qhd,khd->hqk", query_heads, keys_heads, preferred_element_type=jnp.float32)
        * score_scale
    )
    score_drift = (
        jnp.einsum("qhd,khd->hqk", query_drift, keys_heads, preferred_element_type=jnp.float32)
        + jnp.einsum("qhd,khd->hqk", query_heads, keys_drift, preferred_element_type=jnp.float32)
    ) * score_scale
    probabilities = jax.nn.softmax(scores, axis=2)
    weights_low = probabilities.astype(jnp.bfloat16)
    drifted = probabilities * score_drift
    drifted_low = drifted.astype(jnp.bfloat16)
    attended = jnp.einsum(
        "hqk,khd->hqd", weights_low, values_heads, preferred_element_type=jnp.float32
    )
    drift_mean = jnp.sum(drifted, axis=2, keepdims=True)
    attended_drift = (
        jnp.einsum("hqk,khd->hqd", drifted_low, values_heads, preferred_element_type=jnp.float32)
        - drift_mean * attended
        + jnp.einsum("hqk,khd->hqd", weights_low, values_drift, preferred_element_type=jnp.float32)
    )
    attended_low = (
        attended.astype(jnp.bfloat16).transpose(1, 0, 2).reshape(group_rows, heads_local * HEAD_DIM)
    )
    drift_low = (
        attended_drift.astype(jnp.bfloat16)
        .transpose(1, 0, 2)
        .reshape(group_rows, heads_local * HEAD_DIM)
    )
    own_attended, own_drift = (
        lax.all_to_all(attended_low, "seq", split_axis=0, concat_axis=1, tiled=True),
        lax.all_to_all(drift_low, "seq", split_axis=0, concat_axis=1, tiled=True),
    )
    residual_state = stream.astype(jnp.float32) + own_attended.astype(jnp.float32)
    state_tangent = stream_tangent.astype(jnp.float32) + own_drift.astype(jnp.float32)
    inverse = lax.rsqrt(jnp.mean(residual_state * residual_state, axis=1, keepdims=True) + epsilon)
    cross_mean = jnp.mean(residual_state * state_tangent, axis=1, keepdims=True)
    normed = (norm_gain * residual_state * inverse).astype(jnp.bfloat16)
    normed_tangent = (
        norm_gain * inverse * (state_tangent - residual_state * cross_mean * inverse * inverse)
    ).astype(jnp.bfloat16)
    slot_count = expert_count * capacity
    kept_mask = slot_index >= 0
    slot_codes = jnp.where(kept_mask, expert_ids * capacity + slot_index, slot_count)
    row_numbers = lax.broadcasted_iota(jnp.int32, slot_index.shape, 0)
    slot_table = (
        jnp.full((slot_count,), local_rows, jnp.int32).at[slot_codes].set(row_numbers, mode="drop")
    )
    padded = jnp.concatenate((normed, jnp.zeros((1, model_width), jnp.bfloat16)), axis=0)
    padded_tangent = jnp.concatenate(
        (normed_tangent, jnp.zeros((1, model_width), jnp.bfloat16)), axis=0
    )
    packed = padded[slot_table]
    packed_tangent = padded_tangent[slot_table]
    outgoing = jnp.repeat(packed.reshape(expert_count, capacity, model_width), 2, axis=0)
    outgoing_tangent = jnp.repeat(
        packed_tangent.reshape(expert_count, capacity, model_width), 2, axis=0
    )
    arrived, arrived_tangent = (
        lax.all_to_all(outgoing, "exp", split_axis=0, concat_axis=0, tiled=True),
        lax.all_to_all(outgoing_tangent, "exp", split_axis=0, concat_axis=0, tiled=True),
    )
    stacked_rows = jnp.stack(
        (arrived.reshape(-1, model_width), arrived_tangent.reshape(-1, model_width))
    )
    hidden_pair = jnp.einsum(
        "prd,dn->prn",
        stacked_rows,
        lax.all_gather(weight_in, "seq", axis=1, tiled=True),
        preferred_element_type=jnp.float32,
    )
    activated, activated_drift = gelu_pair(hidden_pair[0], hidden_pair[1])
    activated_pair = jnp.stack(
        (activated.astype(jnp.bfloat16), activated_drift.astype(jnp.bfloat16))
    )
    projected = jnp.einsum(
        "prn,nd->prd",
        activated_pair,
        lax.all_gather(weight_out, "seq", axis=0, tiled=True),
        preferred_element_type=jnp.float32,
    )
    projected_low = projected.astype(jnp.bfloat16)
    partial_out = projected_low[0].reshape(arrived.shape)
    partial_drift = projected_low[1].reshape(arrived.shape)
    returned, returned_tangent = (
        lax.all_to_all(partial_out, "exp", split_axis=0, concat_axis=0, tiled=True),
        lax.all_to_all(partial_drift, "exp", split_axis=0, concat_axis=0, tiled=True),
    )
    expert_sums = jnp.sum(
        returned.astype(jnp.float32).reshape(expert_count, 2, capacity, model_width), axis=1
    ).reshape(slot_count, model_width)
    expert_drifts = jnp.sum(
        returned_tangent.astype(jnp.float32).reshape(expert_count, 2, capacity, model_width), axis=1
    ).reshape(slot_count, model_width)
    flat_index = jnp.where(kept_mask, slot_codes, 0)
    gate_values = jnp.where(kept_mask, gate_units.astype(jnp.float32) / 65536.0, 0.0)
    expert_mix = jnp.sum(gate_values[:, :, None] * expert_sums[flat_index], axis=1)
    mix_drift = jnp.sum(gate_values[:, :, None] * expert_drifts[flat_index], axis=1)
    return (
        (residual_state + expert_mix).astype(jnp.bfloat16),
        (state_tangent + mix_drift).astype(jnp.bfloat16),
    )


def solution(mesh):
    return jax.shard_map(
        per_device,
        mesh=mesh,
        in_specs=(
            P(("exp", "seq"), None),
            P(("exp", "seq"), None),
            P(("exp", "seq"), None),
            P(("exp", "seq"), None),
            P(("exp", "seq"), None),
            P(("exp", "seq"), None),
            P(("exp", "seq"), None),
            P(("exp", "seq"), None),
            P(),
            P(("exp", "seq"), None),
            P(("exp", "seq"), None),
            P(("exp", "seq"), None),
            P(None, ("exp", "seq")),
            P(("exp", "seq"), None),
        ),
        out_specs=(P(("exp", "seq"), None), P(("exp", "seq"), None)),
        check_vma=False,
    )
```

profile of v0, /device:TPU:1, one launch (start us, length us, event | category | flops | bytes accessed | tf_op | source)
XLA Modules:
  0.0 295.6 jit_solution(12073281198583563722)
XLA Ops:
  7.9 1.1 copy.32
  9.0 0.9 reshape.239
  9.9 11.8 %all-to-all-start = ((bf16[16,2,2048]{2,1,0:T(2,128)(2,1)}), bf16[16,2,2048]{2,1,0:T(2,128)(2,1)S(1)}, u32[]{:S(2)}, u32[]{:S(2)}) async-start(bf16[16,2,2048]{2,1,0:T(2,128)(2,1)} %reshape.239), calls=%async_computation | async-start | bytes 262144 | tf_op jit(solution)/shard_map/all_to_all | solution.py:50
  21.7 1.1 copy.34
  22.8 0.9 reshape.241
  23.7 7.2 %all-to-all-done = bf16[16,2,2048]{2,1,0:T(2,128)(2,1)S(1)} async-done(((bf16[16,2,2048]{2,1,0:T(2,128)(2,1)}), bf16[16,2,2048]{2,1,0:T(2,128)(2,1)S(1)}, u32[]{:S(2)}, u32[]{:S(2)}) %all-to-all-start) | async-done | bytes 131104 | tf_op jit(solution)/shard_map/all_to_all | solution.py:50
  30.9 3.4 %all-to-all-start.1 = ((bf16[16,2,2048]{2,1,0:T(2,128)(2,1)}), bf16[16,2,2048]{2,1,0:T(2,128)(2,1)S(1)}, u32[]{:S(2)}, u32[]{:S(2)}) async-start(bf16[16,2,2048]{2,1,0:T(2,128)(2,1)} %reshape.241), calls=%async_computation.1 | async-start | bytes 262144 | tf_op jit(solution)/shard_map/all_to_all | solution.py:51
  34.3 1.1 copy.42
  35.4 0.9 reshape.247
  36.3 8.1 %all-to-all-done.1 = bf16[16,2,2048]{2,1,0:T(2,128)(2,1)S(1)} async-done(((bf16[16,2,2048]{2,1,0:T(2,128)(2,1)}), bf16[16,2,2048]{2,1,0:T(2,128)(2,1)S(1)}, u32[]{:S(2)}, u32[]{:S(2)}) %all-to-all-start.1) | async-done | bytes 131104 | tf_op jit(solution)/shard_map/all_to_all | solution.py:51
  44.4 3.7 %all-to-all-start.5 = ((bf16[16,2,2048]{2,1,0:T(2,128)(2,1)}), bf16[16,2,2048]{2,1,0:T(2,128)(2,1)S(1)}, u32[]{:S(2)}, u32[]{:S(2)}) async-start(bf16[16,2,2048]{2,1,0:T(2,128)(2,1)} %reshape.247), calls=%async_computation.5 | async-start | bytes 262144 | tf_op jit(solution)/shard_map/all_to_all | solution.py:53
  48.1 0.7 all-gather.5.cloned.1.call-update
  49.0 0.9 reshape.249
  50.1 0.9 reshape.237
  51.2 0.9 reshape.245
  52.3 6.1 %all-to-all-done.5 = bf16[16,2,2048]{2,1,0:T(2,128)(2,1)S(1)} async-done(((bf16[16,2,2048]{2,1,0:T(2,128)(2,1)}), bf16[16,2,2048]{2,1,0:T(2,128)(2,1)S(1)}, u32[]{:S(2)}, u32[]{:S(2)}) %all-to-all-start.5) | async-done | bytes 131104 | tf_op jit(solution)/shard_map/all_to_all | solution.py:53
  58.4 3.5 %all-to-all-start.6 = ((bf16[16,2,2048]{2,1,0:T(2,128)(2,1)}), bf16[16,2,2048]{2,1,0:T(2,128)(2,1)S(1)}, u32[]{:S(2)}, u32[]{:S(2)}) async-start(bf16[16,2,2048]{2,1,0:T(2,128)(2,1)} %reshape.249), calls=%async_computation.6 | async-start | bytes 262144 | tf_op jit(solution)/shard_map/all_to_all | solution.py:54
  62.4 9.5 %all-to-all-done.6 = bf16[16,2,2048]{2,1,0:T(2,128)(2,1)S(1)} async-done(((bf16[16,2,2048]{2,1,0:T(2,128)(2,1)}), bf16[16,2,2048]{2,1,0:T(2,128)(2,1)S(1)}, u32[]{:S(2)}, u32[]{:S(2)}) %all-to-all-start.6) | async-done | bytes 131104 | tf_op jit(solution)/shard_map/all_to_all | solution.py:54
  71.8 3.4 %all-to-all-start.2 = ((bf16[16,2,2048]{2,1,0:T(2,128)(2,1)}), bf16[16,2,2048]{2,1,0:T(2,128)(2,1)S(1)}, u32[]{:S(2)}, u32[]{:S(2)}) async-start(bf16[16,2,2048]{2,1,0:T(2,128)(2,1)} %reshape.237), calls=%async_computation.2 | async-start | bytes 262144 | tf_op jit(solution)/shard_map/all_to_all | solution.py:52
  77.1 6.6 %all-to-all-done.2 = bf16[16,2,2048]{2,1,0:T(2,128)(2,1)S(1)} async-done(((bf16[16,2,2048]{2,1,0:T(2,128)(2,1)}), bf16[16,2,2048]{2,1,0:T(2,128)(2,1)S(1)}, u32[]{:S(2)}, u32[]{:S(2)}) %all-to-all-start.2) | async-done | bytes 131104 | tf_op jit(solution)/shard_map/all_to_all | solution.py:52
  83.6 3.6 %all-to-all-start.7 = ((bf16[16,2,2048]{2,1,0:T(2,128)(2,1)}), bf16[16,2,2048]{2,1,0:T(2,128)(2,1)S(1)}, u32[]{:S(2)}, u32[]{:S(2)}) async-start(bf16[16,2,2048]{2,1,0:T(2,128)(2,1)} %reshape.245), calls=%async_computation.7 | async-start | bytes 262144 | tf_op jit(solution)/shard_map/all_to_all | solution.py:55
  87.8 2.7 multiply_reduce_fusion
  90.6 2.7 fusion.48
  93.3 2.5 all-to-all-done.7
  96.5 3.2 %fusion.5 = f32[1024]{0:T(1024)S(1)} fusion(f32[1024,1024]{0,1:T(8,128)} %get-tuple-element.15, f32[1024]{0:T(1024)S(1)} %get-tuple-element.14), kind=kLoop, calls=%fused_computation.15 | loop fusion | flops 3144704 | bytes 4202496 | tf_op jit(solution)/shard_map/reduce_sum | solution.py:75
  100.1 1.0 fusion.37
  101.0 1.0 fusion.46
  102.0 1.3 copy-done.1
  103.3 1.5 fusion.47
  105.7 0.9 reshape.251
  106.6 4.4 %all-to-all-start.8 = ((bf16[16,2,2048]{2,1,0:T(2,128)(2,1)}), bf16[16,2,2048]{2,1,0:T(2,128)(2,1)S(1)}, u32[]{:S(2)}, u32[]{:S(2)}) async-start(bf16[16,2,2048]{2,1,0:T(2,128)(2,1)} %reshape.251), calls=%async_computation.8 | async-start | bytes 262144 | tf_op jit(solution)/shard_map/all_to_all | solution.py:98
  111.3 1.0 scatter_custom_fusion
  112.6 0.9 reshape.243
  113.5 6.9 %all-to-all-done.8 = bf16[16,2,2048]{2,1,0:T(2,128)(2,1)S(1)} async-done(((bf16[16,2,2048]{2,1,0:T(2,128)(2,1)}), bf16[16,2,2048]{2,1,0:T(2,128)(2,1)S(1)}, u32[]{:S(2)}, u32[]{:S(2)}) %all-to-all-start.8) | async-done | bytes 131104 | tf_op jit(solution)/shard_map/all_to_all | solution.py:98
  120.5 3.4 %all-to-all-start.3 = ((bf16[16,2,2048]{2,1,0:T(2,128)(2,1)}), bf16[16,2,2048]{2,1,0:T(2,128)(2,1)S(1)}, u32[]{:S(2)}, u32[]{:S(2)}) async-start(bf16[16,2,2048]{2,1,0:T(2,128)(2,1)} %reshape.243), calls=%async_computation.3 | async-start | bytes 262144 | tf_op jit(solution)/shard_map/all_to_all | solution.py:97
  124.4 8.7 %all-to-all-done.3 = bf16[16,2,2048]{2,1,0:T(2,128)(2,1)S(1)} async-done(((bf16[16,2,2048]{2,1,0:T(2,128)(2,1)}), bf16[16,2,2048]{2,1,0:T(2,128)(2,1)S(1)}, u32[]{:S(2)}, u32[]{:S(2)}) %all-to-all-start.3) | async-done | bytes 131104 | tf_op jit(solution)/shard_map/all_to_all | solution.py:97
  134.0 0.9 gather_fusion
  135.0 1.2 broadcast_in_dim.43
  136.2 9.4 %all-to-all-start.4 = ((bf16[32,10,1024]{2,1,0:T(8,128)(2,1)}), bf16[32,10,1024]{2,1,0:T(8,128)(2,1)S(1)}, u32[]{:S(2)}, u32[]{:S(2)}) async-start(bf16[32,10,1024]{2,1,0:T(8,128)(2,1)} %bitcast.8), calls=%async_computation.4 | async-start | bytes 2097152 | tf_op jit(solution)/shard_map/all_to_all | solution.py:126
  145.7 0.9 gather_fusion.1
  146.8 26.2 %all-to-all-done.4 = bf16[32,10,1024]{2,1,0:T(8,128)(2,1)S(1)} async-done(((bf16[32,10,1024]{2,1,0:T(8,128)(2,1)}), bf16[32,10,1024]{2,1,0:T(8,128)(2,1)S(1)}, u32[]{:S(2)}, u32[]{:S(2)}) %all-to-all-start.4) | async-done | bytes 655392 | tf_op jit(solution)/shard_map/all_to_all | solution.py:126
  173.0 1.2 broadcast_in_dim.44
  174.2 6.0 %all-to-all-start.9 = ((bf16[32,10,1024]{2,1,0:T(8,128)(2,1)}), bf16[32,10,1024]{2,1,0:T(8,128)(2,1)S(1)}, u32[]{:S(2)}, u32[]{:S(2)}) async-start(bf16[32,10,1024]{2,1,0:T(8,128)(2,1)} %bitcast.17), calls=%async_computation.9 | async-start | bytes 2097152 | tf_op jit(solution)/shard_map/all_to_all | solution.py:127
  180.1 1.1 stack_reshape.6
  181.2 24.8 %all-to-all-done.9 = bf16[32,10,1024]{2,1,0:T(8,128)(2,1)S(1)} async-done(((bf16[32,10,1024]{2,1,0:T(8,128)(2,1)}), bf16[32,10,1024]{2,1,0:T(8,128)(2,1)S(1)}, u32[]{:S(2)}, u32[]{:S(2)}) %all-to-all-start.9) | async-done | bytes 655392 | tf_op jit(solution)/shard_map/all_to_all | solution.py:127
  206.2 4.8 %fusion.2 = f32[2,320,2048]{2,1,0:T(8,128)S(1)} fusion(bf16[1024,2048]{1,0:T(8,128)(2,1)} %all-gather.3.cloned.1.call-done, bf16[1,320,1024]{2,1,0:T(8,128)(2,1)S(1)} %stack_reshape.7, bf16[1,320,1024]{2,1,0:T(8,128)(2,1)} %stack_reshape.6), kind=kOutput, calls=%fused_computation.7 | convolution fusion | flops 2685009920 | bytes 10747904 | tf_op jit(solution)/shard_map/prd,dn->prn/dot_general | solution.py:132
  211.0 1.8 multiply_convert_fusion
  212.9 5.1 %fusion.18 = bf16[2,320,1024]{2,1,0:T(8,128)(2,1)S(1)} fusion(bf16[2048,1024]{1,0:T(8,128)(2,1)} %all-gather.5.cloned.1.call-done, bf16[1,320,2048]{2,1,0:T(8,128)(2,1)S(1)} %get-tuple-element.7, bf16[1,320,2048]{2,1,0:T(8,128)(2,1)S(1)} %get-tuple-element.6), kind=kOutput, calls=%fused_computation.31 | convolution fusion | flops 2686320640 | bytes 8126464 | tf_op jit(solution)/shard_map/prn,nd->prd/dot_general | solution.py:142
  218.1 1.2 reshape_squeeze.6
  219.3 6.6 %all-to-all-start.10 = ((bf16[32,10,1024]{2,1,0:T(8,128)(2,1)}), bf16[32,10,1024]{2,1,0:T(8,128)(2,1)S(1)}, u32[]{:S(2)}, u32[]{:S(2)}) async-start(bf16[32,10,1024]{2,1,0:T(8,128)(2,1)} %reshape_squeeze.6), calls=%async_computation.10 | async-start | bytes 2097152 | tf_op jit(solution)/shard_map/all_to_all | solution.py:152
  225.9 1.2 reshape_squeeze.7
  227.1 23.5 %all-to-all-done.10 = bf16[32,10,1024]{2,1,0:T(8,128)(2,1)S(1)} async-done(((bf16[32,10,1024]{2,1,0:T(8,128)(2,1)}), bf16[32,10,1024]{2,1,0:T(8,128)(2,1)S(1)}, u32[]{:S(2)}, u32[]{:S(2)}) %all-to-all-start.10) | async-done | bytes 655392 | tf_op jit(solution)/shard_map/all_to_all | solution.py:152
  250.5 7.3 %all-to-all-start.11 = ((bf16[32,10,1024]{2,1,0:T(8,128)(2,1)}), bf16[32,10,1024]{2,1,0:T(8,128)(2,1)S(1)}, u32[]{:S(2)}, u32[]{:S(2)}) async-start(bf16[32,10,1024]{2,1,0:T(8,128)(2,1)} %reshape_squeeze.7), calls=%async_computation.11 | async-start | bytes 2097152 | tf_op jit(solution)/shard_map/all_to_all | solution.py:153
  258.3 1.2 convert_reduce_fusion.1
  259.5 1.3 reshape.175
  260.8 1.6 gather_fusion.2
  262.4 1.3 reshape.202
  263.7 18.6 %all-to-all-done.11 = bf16[32,10,1024]{2,1,0:T(8,128)(2,1)S(1)} async-done(((bf16[32,10,1024]{2,1,0:T(8,128)(2,1)}), bf16[32,10,1024]{2,1,0:T(8,128)(2,1)S(1)}, u32[]{:S(2)}, u32[]{:S(2)}) %all-to-all-start.11) | async-done | bytes 655392 | tf_op jit(solution)/shard_map/all_to_all | solution.py:153
  282.3 1.2 convert_reduce_fusion
  283.5 1.3 reshape.178
  284.8 0.8 gather_fusion.3
  286.0 1.4 multiply_reduce_fusion.1
  287.4 0.7 add_convert_fusion
  288.1 0.7 add_convert_fusion.1
  (86 shorter events, 9.3 us)
Async XLA Ops:
  7.2 41.7 %copy-start.4 = (bf16[64,1024]{1,0:T(8,128)(2,1)S(1)}, bf16[64,1024]{1,0:T(8,128)(2,1)}, u32[]{:S(2)}) copy-start(bf16[64,1024]{1,0:T(8,128)(2,1)} %param.18) | copy-start | bytes 393220
  7.2 42.7 %copy-start.5 = (bf16[64,1024]{1,0:T(8,128)(2,1)S(1)}, bf16[64,1024]{1,0:T(8,128)(2,1)}, u32[]{:S(2)}) copy-start(bf16[64,1024]{1,0:T(8,128)(2,1)} %param.16) | copy-start | bytes 393220
  7.2 43.8 %copy-start.6 = (bf16[64,1024]{1,0:T(8,128)(2,1)S(1)}, bf16[64,1024]{1,0:T(8,128)(2,1)}, u32[]{:S(2)}) copy-start(bf16[64,1024]{1,0:T(8,128)(2,1)} %param.19) | copy-start | bytes 393220
  7.2 199.0 %all-gather.3.cloned.1.call-start = ((), (), s32[]{:S(2)}) async-start(), calls=%async_computation.12 | async-start | bytes 4456448 | tf_op jit(solution)/shard_map/all_gather | solution.py:135
  9.9 21.0 %all-to-all-start = ((bf16[16,2,2048]{2,1,0:T(2,128)(2,1)}), bf16[16,2,2048]{2,1,0:T(2,128)(2,1)S(1)}, u32[]{:S(2)}, u32[]{:S(2)}) async-start(bf16[16,2,2048]{2,1,0:T(2,128)(2,1)} %reshape.239), calls=%async_computation | async-start | bytes 262144 | tf_op jit(solution)/shard_map/all_to_all | solution.py:50
  30.9 13.5 %all-to-all-start.1 = ((bf16[16,2,2048]{2,1,0:T(2,128)(2,1)}), bf16[16,2,2048]{2,1,0:T(2,128)(2,1)S(1)}, u32[]{:S(2)}, u32[]{:S(2)}) async-start(bf16[16,2,2048]{2,1,0:T(2,128)(2,1)} %reshape.241), calls=%async_computation.1 | async-start | bytes 262144 | tf_op jit(solution)/shard_map/all_to_all | solution.py:51
  44.4 14.0 %all-to-all-start.5 = ((bf16[16,2,2048]{2,1,0:T(2,128)(2,1)}), bf16[16,2,2048]{2,1,0:T(2,128)(2,1)S(1)}, u32[]{:S(2)}, u32[]{:S(2)}) async-start(bf16[16,2,2048]{2,1,0:T(2,128)(2,1)} %reshape.247), calls=%async_computation.5 | async-start | bytes 262144 | tf_op jit(solution)/shard_map/all_to_all | solution.py:53
  48.1 164.8 %all-gather.5.cloned.1.call-start = ((), (), s32[]{:S(2)}) async-start(), calls=%async_computation.13 | async-start | bytes 4456448 | tf_op jit(solution)/shard_map/all_gather | solution.py:145
  58.4 13.4 %all-to-all-start.6 = ((bf16[16,2,2048]{2,1,0:T(2,128)(2,1)}), bf16[16,2,2048]{2,1,0:T(2,128)(2,1)S(1)}, u32[]{:S(2)}, u32[]{:S(2)}) async-start(bf16[16,2,2048]{2,1,0:T(2,128)(2,1)} %reshape.249), calls=%async_computation.6 | async-start | bytes 262144 | tf_op jit(solution)/shard_map/all_to_all | solution.py:54
  71.8 11.8 %all-to-all-start.2 = ((bf16[16,2,2048]{2,1,0:T(2,128)(2,1)}), bf16[16,2,2048]{2,1,0:T(2,128)(2,1)S(1)}, u32[]{:S(2)}, u32[]{:S(2)}) async-start(bf16[16,2,2048]{2,1,0:T(2,128)(2,1)} %reshape.237), calls=%async_computation.2 | async-start | bytes 262144 | tf_op jit(solution)/shard_map/all_to_all | solution.py:52
  83.6 12.2 %all-to-all-start.7 = ((bf16[16,2,2048]{2,1,0:T(2,128)(2,1)}), bf16[16,2,2048]{2,1,0:T(2,128)(2,1)S(1)}, u32[]{:S(2)}, u32[]{:S(2)}) async-start(bf16[16,2,2048]{2,1,0:T(2,128)(2,1)} %reshape.245), calls=%async_computation.7 | async-start | bytes 262144 | tf_op jit(solution)/shard_map/all_to_all | solution.py:55
  96.4 3.6 %copy-start = (f32[1024,1024]{0,1:T(8,128)S(1)}, f32[1024,1024]{0,1:T(8,128)}, u32[]{:S(2)}) copy-start(f32[1024,1024]{0,1:T(8,128)} %get-tuple-element.15) | copy-start | bytes 12582916
  101.0 2.3 copy-start.1
  104.8 6.1 %copy-start.8 = (s32[64,2]{0,1:T(2,128)S(1)}, s32[64,2]{0,1:T(2,128)}, u32[]{:S(2)}) copy-start(s32[64,2]{0,1:T(2,128)} %param.25) | copy-start | bytes 1540
  104.9 6.1 %copy-start.10 = (s32[64,2]{0,1:T(2,128)S(1)}, s32[64,2]{0,1:T(2,128)}, u32[]{:S(2)}) copy-start(s32[64,2]{0,1:T(2,128)} %param.23) | copy-start | bytes 1540
  106.6 13.9 %all-to-all-start.8 = ((bf16[16,2,2048]{2,1,0:T(2,128)(2,1)}), bf16[16,2,2048]{2,1,0:T(2,128)(2,1)S(1)}, u32[]{:S(2)}, u32[]{:S(2)}) async-start(bf16[16,2,2048]{2,1,0:T(2,128)(2,1)} %reshape.251), calls=%async_computation.8 | async-start | bytes 262144 | tf_op jit(solution)/shard_map/all_to_all | solution.py:98
  112.5 21.0 %copy-start.2 = (bf16[64,1024]{1,0:T(8,128)(2,1)S(1)}, bf16[64,1024]{1,0:T(8,128)(2,1)}, u32[]{:S(2)}) copy-start(bf16[64,1024]{1,0:T(8,128)(2,1)} %param.21) | copy-start | bytes 393220
  112.5 21.0 %copy-start.3 = (bf16[64,1024]{1,0:T(8,128)(2,1)S(1)}, bf16[64,1024]{1,0:T(8,128)(2,1)}, u32[]{:S(2)}) copy-start(bf16[64,1024]{1,0:T(8,128)(2,1)} %param.20) | copy-start | bytes 393220
  112.6 21.1 %copy-start.7 = (f32[1024]{0:T(1024)S(1)}, f32[1024]{0:T(1024)}, u32[]{:S(2)}) copy-start(f32[1024]{0:T(1024)} %param.22) | copy-start | bytes 12292
  120.5 12.6 %all-to-all-start.3 = ((bf16[16,2,2048]{2,1,0:T(2,128)(2,1)}), bf16[16,2,2048]{2,1,0:T(2,128)(2,1)S(1)}, u32[]{:S(2)}, u32[]{:S(2)}) async-start(bf16[16,2,2048]{2,1,0:T(2,128)(2,1)} %reshape.243), calls=%async_computation.3 | async-start | bytes 262144 | tf_op jit(solution)/shard_map/all_to_all | solution.py:97
  136.2 36.8 %all-to-all-start.4 = ((bf16[32,10,1024]{2,1,0:T(8,128)(2,1)}), bf16[32,10,1024]{2,1,0:T(8,128)(2,1)S(1)}, u32[]{:S(2)}, u32[]{:S(2)}) async-start(bf16[32,10,1024]{2,1,0:T(8,128)(2,1)} %bitcast.8), calls=%async_computation.4 | async-start | bytes 2097152 | tf_op jit(solution)/shard_map/all_to_all | solution.py:126
  174.2 31.8 %all-to-all-start.9 = ((bf16[32,10,1024]{2,1,0:T(8,128)(2,1)}), bf16[32,10,1024]{2,1,0:T(8,128)(2,1)S(1)}, u32[]{:S(2)}, u32[]{:S(2)}) async-start(bf16[32,10,1024]{2,1,0:T(8,128)(2,1)} %bitcast.17), calls=%async_computation.9 | async-start | bytes 2097152 | tf_op jit(solution)/shard_map/all_to_all | solution.py:127
  219.3 38.9 %copy-start.9 = (s32[64,2]{0,1:T(2,128)S(1)}, s32[64,2]{0,1:T(2,128)}, u32[]{:S(2)}) copy-start(s32[64,2]{0,1:T(2,128)} %param.24) | copy-start | bytes 1540
  219.3 31.3 %all-to-all-start.10 = ((bf16[32,10,1024]{2,1,0:T(8,128)(2,1)}), bf16[32,10,1024]{2,1,0:T(8,128)(2,1)S(1)}, u32[]{:S(2)}, u32[]{:S(2)}) async-start(bf16[32,10,1024]{2,1,0:T(8,128)(2,1)} %reshape_squeeze.6), calls=%async_computation.10 | async-start | bytes 2097152 | tf_op jit(solution)/shard_map/all_to_all | solution.py:152
  250.5 31.7 %all-to-all-start.11 = ((bf16[32,10,1024]{2,1,0:T(8,128)(2,1)}), bf16[32,10,1024]{2,1,0:T(8,128)(2,1)S(1)}, u32[]{:S(2)}, u32[]{:S(2)}) async-start(bf16[32,10,1024]{2,1,0:T(8,128)(2,1)} %reshape_squeeze.7), calls=%async_computation.11 | async-start | bytes 2097152 | tf_op jit(solution)/shard_map/all_to_all | solution.py:153
Sparse Core Ops, SparseCore 0:
  10.1 66.4 all-gather.2
  78.7 45.4 all-gather.4
where the time goes:
time: 300 us; the launch traced here: 296 us
  waiting for transfers between devices  150 us (50%)
  starting transfers between devices  66.6 us (22%)
  local copies, waits for them, and re-layouts  34.3 us (11%)
  matrix products  19.3 us (6%)
  between operations  14.7 us (5%)
  other arithmetic  10.7 us (4%)
    all_to_all x1, waiting for transfers between devices, per_device(): lax.all_to_all(outgoing, 'exp', split_axis=0, concat_axis=0, tiled=True)  26.2 us
    all_to_all x1, waiting for transfers between devices, per_device(): lax.all_to_all(outgoing_tangent, 'exp', split_axis=0, concat_axis=0, tile...  24.8 us
    all_to_all x1, waiting for transfers between devices, per_device(): lax.all_to_all(partial_out, 'exp', split_axis=0, concat_axis=0, tiled=True)  23.5 us
    all_to_all x1, waiting for transfers between devices, per_device(): lax.all_to_all(partial_drift, 'exp', split_axis=0, concat_axis=0, tiled=T...  18.6 us
    unnamed x44, local copies, waits for them, and re-layouts  14.4 us
    all_to_all x1, starting transfers between devices, per_device(): lax.all_to_all(query_rows, 'seq', split_axis=1, concat_axis=0, tiled=True)  11.8 us
    all_to_all x1, waiting for transfers between devices, per_device(): lax.all_to_all(key_tangent, 'seq', split_axis=1, concat_axis=0, tiled=True)  9.45 us
    all_to_all x1, starting transfers between devices, per_device(): lax.all_to_all(outgoing, 'exp', split_axis=0, concat_axis=0, tiled=True)  9.44 us
  transfers between devices with their start and end apart: 14, of which 12 were waited for; matrix products, arithmetic and copies ran while one was open for 17% of the time, Pallas kernels for 0%

commit v1 on v0

v1 whole, which is shorter than its diff:
```python
import functools

import jax
import jax.numpy as jnp
from jax import lax
from jax.experimental import pallas as pl
from jax.experimental.pallas import tpu as pltpu
from jax.sharding import PartitionSpec as P

MESH = pl.DeviceIdType.MESH
HEAD_DIM = 64
BF16 = jnp.bfloat16
F32 = jnp.float32

epsilon = 1e-06
gelu_coef = 0.7978845608028654
cubic_coef = 0.044715


def gelu_pair(inputs, tangent):
    inner_arg = gelu_coef * (inputs + cubic_coef * inputs * inputs * inputs)
    hyperbolic = jnp.tanh(inner_arg)
    values = 0.5 * inputs * (1.0 + hyperbolic)
    slopes = 0.5 * (1.0 + hyperbolic) + 0.5 * inputs * (
        1.0 - hyperbolic * hyperbolic
    ) * gelu_coef * (1.0 + 3.0 * cubic_coef * inputs * inputs)
    return (values, slopes * tangent)


def dot(a, b):
    return jnp.dot(a, b, preferred_element_type=F32)


def attention_kernel(
    n,
    q,
    k,
    v,
    dq,
    dk,
    dv,
    stream,
    stream_tangent,
    gain,
    state_out,
    tangent_out,
    normed_out,
    normed_tangent_out,
    x_send,
    yz_send,
    x_all,
    yz_all,
    k_top,
    k_low,
    z_low,
    o_send,
    o_all,
    x_sent,
    x_came,
    yz_sent,
    yz_came,
    o_sent,
    o_came,
):
    rows = q.shape[0]
    me = lax.axis_index("seq")
    barrier = pltpu.get_barrier_semaphore()

    def greet(j, carry):
        pl.semaphore_signal(
            barrier, inc=1, device_id={"seq": lax.rem(me + j, n)}, device_id_type=MESH
        )
        return carry

    lax.fori_loop(1, n, greet, 0)
    for h in range(n):
        cols = slice(h * HEAD_DIM, (h + 1) * HEAD_DIM)
        x_send[h] = jnp.concatenate((dq[:, cols], q[:, cols]), axis=1) * BF16(HEAD_DIM**-0.5)
        yz_send[h] = jnp.concatenate((k[:, cols], dk[:, cols], v[:, cols], dv[:, cols]), axis=1)
    pl.semaphore_wait(barrier, n - 1)

    def part(index):
        return pl.ds(pl.multiple_of(index * rows, rows), rows)

    def yz_copy(dest, slot):
        return pltpu.make_async_remote_copy(
            src_ref=yz_send.at[dest],
            dst_ref=yz_all.at[part(slot)],
            send_sem=yz_sent.at[dest],
            recv_sem=yz_came.at[slot],
            device_id={"seq": dest},
            device_id_type=MESH,
        )

    def x_copy(dest, slot):
        return pltpu.make_async_remote_copy(
            src_ref=x_send.at[dest],
            dst_ref=x_all.at[part(slot)],
            send_sem=x_sent.at[dest],
            recv_sem=x_came.at[slot],
            device_id={"seq": dest},
            device_id_type=MESH,
        )

    def o_copy(dest, slot):
        return pltpu.make_async_remote_copy(
            src_ref=o_send.at[part(dest)],
            dst_ref=o_all.at[slot],
            send_sem=o_sent.at[dest],
            recv_sem=o_came.at[slot],
            device_id={"seq": dest},
            device_id_type=MESH,
        )

    for make in (yz_copy, x_copy):

        def send(j, carry):
            make(lax.rem(me + j, n), me).start()
            make(lax.rem(me + n - j, n), me).start()
            return carry

        lax.fori_loop(1, n // 2, send, 0)
        make(lax.rem(me + n // 2, n), me).start()

    yz_all[part(me)] = yz_send[me]
    x_all[part(me)] = x_send[me]

    def yz_arrive(j, carry):
        other = lax.rem(me + j, n)
        yz_copy(other, other).wait_recv()
        return carry

    lax.fori_loop(1, n, yz_arrive, 0)
    turned = yz_all[:, : 2 * HEAD_DIM].T
    k_low[...] = turned
    k_top[:HEAD_DIM] = jnp.zeros_like(turned[:HEAD_DIM])
    k_top[HEAD_DIM:] = turned[:HEAD_DIM]
    z_low[...] = jnp.concatenate(
        (
            jnp.zeros((n * rows, HEAD_DIM), BF16),
            yz_all[:, 2 * HEAD_DIM : 3 * HEAD_DIM],
        ),
        axis=1,
    )
    per = 4
    blocks = n // per
    for i in range(blocks):
        block = lax.rem(me // per + i, blocks)
        for u in range(per):
            other = block * per + u

            @pl.when(other != me)
            def _():
                x_copy(other, other).wait_recv()

        span = pl.ds(pl.multiple_of(block * per * rows, per * rows), per * rows)
        x = x_all[span]
        scores = dot(x, k_top[...])
        drift = dot(x, k_low[...])
        weights = jnp.exp(scores - jnp.max(scores, axis=1, keepdims=True))
        weights = weights * (1.0 / jnp.sum(weights, axis=1, keepdims=True))
        drifted = weights * drift
        mean = jnp.sum(drifted, axis=1, keepdims=True)
        both = dot(weights.astype(BF16), yz_all[:, 2 * HEAD_DIM :])
        low = dot(drifted.astype(BF16), z_low[...])
        attended = both[:, :HEAD_DIM]
        moved = low[:, HEAD_DIM:] - mean * attended + both[:, HEAD_DIM:]
        o_send[span] = jnp.concatenate((attended, moved), axis=1).astype(BF16)
        for u in range(per):
            other = block * per + u

            @pl.when(other != me)
            def _():
                o_copy(other, me).start()

    o_all[me] = o_send[part(me)]

    def o_arrive(j, carry):
        other = lax.rem(me + j, n)
        o_copy(other, other).wait_recv()
        return carry

    lax.fori_loop(1, n, o_arrive, 0)
    for h in range(0, n, 2):
        cols = slice(h * HEAD_DIM, (h + 2) * HEAD_DIM)
        first = o_all[h].astype(F32)
        second = o_all[h + 1].astype(F32)
        state_out[:, cols] = stream[:, cols].astype(F32) + jnp.concatenate(
            (first[:, :HEAD_DIM], second[:, :HEAD_DIM]), axis=1
        )
        tangent_out[:, cols] = stream_tangent[:, cols].astype(F32) + jnp.concatenate(
            (first[:, HEAD_DIM:], second[:, HEAD_DIM:]), axis=1
        )
    state = state_out[...]
    tangent = tangent_out[...]
    inverse = lax.rsqrt(jnp.mean(state * state, axis=1, keepdims=True) + epsilon)
    cross = jnp.mean(state * tangent, axis=1, keepdims=True)
    normed_out[...] = (gain[...] * state * inverse).astype(BF16)
    normed_tangent_out[...] = (
        gain[...] * inverse * (tangent - state * cross * inverse * inverse)
    ).astype(BF16)

    def drain(j, carry):
        other = lax.rem(me + j, n)
        yz_copy(other, me).wait_send()
        x_copy(other, me).wait_send()
        o_copy(other, me).wait_send()
        return carry

    lax.fori_loop(1, n, drain, 0)


def attend(q, k, v, dq, dk, dv, stream, stream_tangent, gain):
    n = lax.axis_size("seq")
    rows, width = stream.shape
    total = n * rows
    vmem = pl.BlockSpec(memory_space=pltpu.VMEM)
    dma = pltpu.SemaphoreType.DMA
    return pl.pallas_call(
        functools.partial(attention_kernel, n),
        out_shape=(
            jax.ShapeDtypeStruct((rows, width), F32),
            jax.ShapeDtypeStruct((rows, width), F32),
            jax.ShapeDtypeStruct((rows, width), BF16),
            jax.ShapeDtypeStruct((rows, width), BF16),
        ),
        in_specs=[vmem] * 9,
        out_specs=(vmem,) * 4,
        scratch_shapes=[
            pltpu.VMEM((n, rows, 2 * HEAD_DIM), BF16),
            pltpu.VMEM((n, rows, 4 * HEAD_DIM), BF16),
            pltpu.VMEM((total, 2 * HEAD_DIM), BF16),
            pltpu.VMEM((total, 4 * HEAD_DIM), BF16),
            pltpu.VMEM((2 * HEAD_DIM, total), BF16),
            pltpu.VMEM((2 * HEAD_DIM, total), BF16),
            pltpu.VMEM((total, 2 * HEAD_DIM), BF16),
            pltpu.VMEM((total, 2 * HEAD_DIM), BF16),
            pltpu.VMEM((n, rows, 2 * HEAD_DIM), BF16),
        ]
        + [dma((n,))] * 6,
        compiler_params=pltpu.CompilerParams(
            collective_id=0, has_side_effects=True, vmem_limit_bytes=48 * 1024 * 1024
        ),
        name="attend",
    )(q, k, v, dq, dk, dv, stream, stream_tangent, gain.reshape(1, width))


def per_device(
    query_rows,
    key_rows,
    value_rows,
    query_tangent,
    key_tangent,
    value_tangent,
    stream,
    stream_tangent,
    norm_gain,
    expert_ids,
    gate_units,
    slot_index,
    weight_in,
    weight_out,
):
    exp_count = lax.axis_size("exp")
    local_rows = stream.shape[0]
    model_width = stream.shape[1]
    expert_count = exp_count // 2
    capacity = 2 * ((5 * local_rows + 4 * expert_count - 1) // (4 * expert_count))
    residual_state, state_tangent, normed, normed_tangent = attend(
        query_rows,
        key_rows,
        value_rows,
        query_tangent,
        key_tangent,
        value_tangent,
        stream,
        stream_tangent,
        norm_gain,
    )
    slot_count = expert_count * capacity
    kept_mask = slot_index >= 0
    slot_codes = jnp.where(kept_mask, expert_ids * capacity + slot_index, slot_count)
    row_numbers = lax.broadcasted_iota(jnp.int32, slot_index.shape, 0)
    slot_table = (
        jnp.full((slot_count,), local_rows, jnp.int32).at[slot_codes].set(row_numbers, mode="drop")
    )
    padded = jnp.concatenate((normed, jnp.zeros((1, model_width), jnp.bfloat16)), axis=0)
    padded_tangent = jnp.concatenate(
        (normed_tangent, jnp.zeros((1, model_width), jnp.bfloat16)), axis=0
    )
    packed = padded[slot_table]
    packed_tangent = padded_tangent[slot_table]
    outgoing = jnp.repeat(packed.reshape(expert_count, capacity, model_width), 2, axis=0)
    outgoing_tangent = jnp.repeat(
        packed_tangent.reshape(expert_count, capacity, model_width), 2, axis=0
    )
    arrived, arrived_tangent = (
        lax.all_to_all(outgoing, "exp", split_axis=0, concat_axis=0, tiled=True),
        lax.all_to_all(outgoing_tangent, "exp", split_axis=0, concat_axis=0, tiled=True),
    )
    stacked_rows = jnp.stack(
        (arrived.reshape(-1, model_width), arrived_tangent.reshape(-1, model_width))
    )
    hidden_pair = jnp.einsum(
        "prd,dn->prn",
        stacked_rows,
        lax.all_gather(weight_in, "seq", axis=1, tiled=True),
        preferred_element_type=jnp.float32,
    )
    activated, activated_drift = gelu_pair(hidden_pair[0], hidden_pair[1])
    activated_pair = jnp.stack(
        (activated.astype(jnp.bfloat16), activated_drift.astype(jnp.bfloat16))
    )
    projected = jnp.einsum(
        "prn,nd->prd",
        activated_pair,
        lax.all_gather(weight_out, "seq", axis=0, tiled=True),
        preferred_element_type=jnp.float32,
    )
    projected_low = projected.astype(jnp.bfloat16)
    partial_out = projected_low[0].reshape(arrived.shape)
    partial_drift = projected_low[1].reshape(arrived.shape)
    returned, returned_tangent = (
        lax.all_to_all(partial_out, "exp", split_axis=0, concat_axis=0, tiled=True),
        lax.all_to_all(partial_drift, "exp", split_axis=0, concat_axis=0, tiled=True),
    )
    expert_sums = jnp.sum(
        returned.astype(jnp.float32).reshape(expert_count, 2, capacity, model_width), axis=1
    ).reshape(slot_count, model_width)
    expert_drifts = jnp.sum(
        returned_tangent.astype(jnp.float32).reshape(expert_count, 2, capacity, model_width), axis=1
    ).reshape(slot_count, model_width)
    flat_index = jnp.where(kept_mask, slot_codes, 0)
    gate_values = jnp.where(kept_mask, gate_units.astype(jnp.float32) / 65536.0, 0.0)
    expert_mix = jnp.sum(gate_values[:, :, None] * expert_sums[flat_index], axis=1)
    mix_drift = jnp.sum(gate_values[:, :, None] * expert_drifts[flat_index], axis=1)
    return (
        (residual_state + expert_mix).astype(jnp.bfloat16),
        (state_tangent + mix_drift).astype(jnp.bfloat16),
    )


def solution(mesh):
    rows = P(("exp", "seq"), None)
    return jax.shard_map(
        per_device,
        mesh=mesh,
        in_specs=(rows,) * 8 + (P(),) + (rows,) * 3 + (P(None, ("exp", "seq")), rows),
        out_specs=(rows, rows),
        check_vma=False,
    )
```

time: 300 us -> 231 us (0.77)
  waiting for transfers between devices: 150 us -> 97.7 us
  Pallas kernels: 0 us -> 46.6 us
  starting transfers between devices: 66.6 us -> 29.5 us
  local copies, waits for them, and re-layouts: 34.3 us -> 21.9 us
  matrix products: 19.3 us -> 9.73 us
  other arithmetic: 10.7 us -> 7.23 us
    all_to_all x8 -> x0, waiting for transfers between devices: 55.6 us -> none  [the longest x1 9.45 us: per_device(): lax.all_to_all(key_tangent, 'seq', split_axis=1, concat_axis=0, tiled=True)]
    pallas_call x0 -> x1, Pallas kernels: none -> 46.6 us  [attend(): pl.pallas_call(functools.partial(attention_kernel, n), out_shape=(jax.Sha...]
    all_to_all x8 -> x0, starting transfers between devices: 37.2 us -> none  [the longest x1 11.8 us: per_device(): lax.all_to_all(query_rows, 'seq', split_axis=1, concat_axis=0, tiled=True)]
    dot_general x6 -> x0, matrix products: 9.4 us -> none  [the longest x1 2.73 us: per_device(): jnp.einsum('qhd,khd->hqk', query_heads, keys_heads, preferred_element_typ...]
    unnamed x44 -> x22, local copies, waits for them, and re-layouts: 14.4 us -> 7.92 us
    reduce_sum x2 -> x0, other arithmetic: 3.34 us -> none  [the longest x1 3.16 us: per_device(): probabilities = jax.nn.softmax(scores, axis=2)]
  transfers between devices with their start and end apart: 14 -> 6, of which waited for: 12 -> 4; matrix products, arithmetic and copies ran while one was open for 17% -> 8% of each run, Pallas kernels for 0% -> 21%
where the time goes in v1:
time: 231 us; the launch traced here: 227 us
  waiting for transfers between devices  97.7 us (42%)
  Pallas kernels  46.6 us (20%)
  starting transfers between devices  29.5 us (13%)
  local copies, waits for them, and re-layouts  21.9 us (9%)
  between operations  14.3 us (6%)
  matrix products  9.73 us (4%)
  other arithmetic  7.23 us (3%)
    pallas_call x1, Pallas kernels, attend(): pl.pallas_call(functools.partial(attention_kernel, n), out_shape=(jax.Sha...  46.6 us
    all_to_all x1, waiting for transfers between devices, per_device(): lax.all_to_all(outgoing, 'exp', split_axis=0, concat_axis=0, tiled=True)  27.1 us
    all_to_all x1, waiting for transfers between devices, per_device(): lax.all_to_all(outgoing_tangent, 'exp', split_axis=0, concat_axis=0, tile...  25.4 us
    all_to_all x1, waiting for transfers between devices, per_device(): lax.all_to_all(partial_out, 'exp', split_axis=0, concat_axis=0, tiled=True)  23.5 us
    all_to_all x1, waiting for transfers between devices, per_device(): lax.all_to_all(partial_drift, 'exp', split_axis=0, concat_axis=0, tiled=T...  20.3 us
    all_to_all x1, starting transfers between devices, per_device(): lax.all_to_all(outgoing, 'exp', split_axis=0, concat_axis=0, tiled=True)  10.1 us
    unnamed x22, local copies, waits for them, and re-layouts  7.92 us
    all_to_all x1, starting transfers between devices, per_device(): lax.all_to_all(partial_drift, 'exp', split_axis=0, concat_axis=0, tiled=T...  7.34 us
  transfers between devices with their start and end apart: 6, of which 4 were waited for; matrix products, arithmetic and copies ran while one was open for 8% of the time, Pallas kernels for 21%

profile of v1, /device:TPU:1, one launch (start us, length us, event | category | flops | bytes accessed | tf_op | source)
XLA Modules:
  0.0 227.0 jit_solution(9562606946838237043)
XLA Ops:
  7.2 0.0 all-gather.3.cloned.1.call-start
  7.2 0.7 all-gather.3.cloned.1.call-update
  7.9 0.0 all-gather.5.cloned.1.call-start
  7.9 0.7 all-gather.5.cloned.1.call-update
  8.6 0.7 compare_select_fusion
  9.4 0.1 copy.20
  9.4 0.1 reshape.87
  9.6 0.1 reshape.89
  9.7 0.0 copy-start
  9.8 0.9 copy-done
  10.6 0.0 copy-start.1
  10.7 0.9 copy-done.1
  11.6 0.0 copy-start.2
  11.6 0.9 copy-done.2
  12.5 0.0 copy-start.3
  12.5 0.9 copy-done.3
  13.4 0.0 copy-start.4
  13.4 0.9 copy-done.4
  14.3 0.0 copy-start.5
  14.3 0.9 copy-done.5
  15.2 0.9 copy-done.6
  16.1 0.9 copy-done.7
  17.0 0.7 copy-done.8
  17.7 46.6 %attend.1 = (f32[64,1024]{1,0:T(8,128)S(1)}, f32[64,1024]{1,0:T(8,128)S(1)}, bf16[64,1024]{1,0:T(8,128)(2,1)S(1)}, bf16[64,1024]{1,0:T(8,128)(2,1)S(1)}) custom-call(bf16[64,1024]{1,0:T(8,128)(2,1)S(1)} %copy-done, bf16[64,1024]{1,0:T(8,128)(2,1)S(1)} %copy-done.1, bf16[64,1024]{1,0:T(8,128)(2,1)S(1)} %copy-done.2, bf16[64,1024]{1,0:T(8,128)(2,1)S(1)} %copy-done.3, ...), custom_call_target="tpu_custom_call" | custom-call | tf_op jit(solution)/shard_map/attend/pallas_call | solution.py:219
  64.3 1.0 scatter_custom_fusion
  65.3 0.9 gather_fusion
  66.3 0.1 reshape.39
  66.4 1.2 broadcast_in_dim.36
  67.6 10.1 %all-to-all-start = ((bf16[32,10,1024]{2,1,0:T(8,128)(2,1)}), bf16[32,10,1024]{2,1,0:T(8,128)(2,1)S(1)}, u32[]{:S(2)}, u32[]{:S(2)}) async-start(bf16[32,10,1024]{2,1,0:T(8,128)(2,1)} %bitcast.1), calls=%async_computation | async-start | bytes 2097152 | tf_op jit(solution)/shard_map/all_to_all | solution.py:298
  77.7 0.9 gather_fusion.1
  78.7 0.1 reshape.41
  78.8 27.1 %all-to-all-done = bf16[32,10,1024]{2,1,0:T(8,128)(2,1)S(1)} async-done(((bf16[32,10,1024]{2,1,0:T(8,128)(2,1)}), bf16[32,10,1024]{2,1,0:T(8,128)(2,1)S(1)}, u32[]{:S(2)}, u32[]{:S(2)}) %all-to-all-start) | async-done | bytes 655392 | tf_op jit(solution)/shard_map/all_to_all | solution.py:298
  105.9 1.2 broadcast_in_dim.37
  107.1 5.3 %all-to-all-start.1 = ((bf16[32,10,1024]{2,1,0:T(8,128)(2,1)}), bf16[32,10,1024]{2,1,0:T(8,128)(2,1)S(1)}, u32[]{:S(2)}, u32[]{:S(2)}) async-start(bf16[32,10,1024]{2,1,0:T(8,128)(2,1)} %bitcast.2), calls=%async_computation.1 | async-start | bytes 2097152 | tf_op jit(solution)/shard_map/all_to_all | solution.py:299
  112.4 0.2 stack_reshape.6
  112.6 25.4 %all-to-all-done.1 = bf16[32,10,1024]{2,1,0:T(8,128)(2,1)S(1)} async-done(((bf16[32,10,1024]{2,1,0:T(8,128)(2,1)}), bf16[32,10,1024]{2,1,0:T(8,128)(2,1)S(1)}, u32[]{:S(2)}, u32[]{:S(2)}) %all-to-all-start.1) | async-done | bytes 655392 | tf_op jit(solution)/shard_map/all_to_all | solution.py:299
  138.0 0.2 stack_reshape.7
  138.2 0.0 all-gather.3.cloned.1.call-done
  138.2 4.7 %fusion.2 = f32[2,320,2048]{2,1,0:T(8,128)S(1)} fusion(bf16[1024,2048]{1,0:T(8,128)(2,1)} %all-gather.3.cloned.1.call-done, bf16[1,320,1024]{2,1,0:T(8,128)(2,1)S(1)} %stack_reshape.7, bf16[1,320,1024]{2,1,0:T(8,128)(2,1)S(1)} %stack_reshape.6), kind=kOutput, calls=%fused_computation.7 | convolution fusion | flops 2685009920 | bytes 10747904 | tf_op jit(solution)/shard_map/prd,dn->prn/dot_general | solution.py:304
  142.9 1.8 multiply_convert_fusion
  144.8 0.0 all-gather.5.cloned.1.call-done
  144.8 5.1 %fusion.14 = bf16[2,320,1024]{2,1,0:T(8,128)(2,1)S(1)} fusion(bf16[2048,1024]{1,0:T(8,128)(2,1)} %all-gather.5.cloned.1.call-done, bf16[1,320,2048]{2,1,0:T(8,128)(2,1)S(1)} %get-tuple-element.13, bf16[1,320,2048]{2,1,0:T(8,128)(2,1)S(1)} %get-tuple-element.12), kind=kOutput, calls=%fused_computation.24 | convolution fusion | flops 2686320640 | bytes 8126464 | tf_op jit(solution)/shard_map/prn,nd->prd/dot_general | solution.py:314
  149.9 0.1 fusion.26
  150.0 1.2 reshape_squeeze.6
  151.2 6.7 %all-to-all-start.2 = ((bf16[32,10,1024]{2,1,0:T(8,128)(2,1)}), bf16[32,10,1024]{2,1,0:T(8,128)(2,1)S(1)}, u32[]{:S(2)}, u32[]{:S(2)}) async-start(bf16[32,10,1024]{2,1,0:T(8,128)(2,1)} %reshape_squeeze.6), calls=%async_computation.2 | async-start | bytes 2097152 | tf_op jit(solution)/shard_map/all_to_all | solution.py:324
  157.8 1.2 reshape_squeeze.7
  159.0 23.5 %all-to-all-done.2 = bf16[32,10,1024]{2,1,0:T(8,128)(2,1)S(1)} async-done(((bf16[32,10,1024]{2,1,0:T(8,128)(2,1)}), bf16[32,10,1024]{2,1,0:T(8,128)(2,1)S(1)}, u32[]{:S(2)}, u32[]{:S(2)}) %all-to-all-start.2) | async-done | bytes 655392 | tf_op jit(solution)/shard_map/all_to_all | solution.py:324
  182.5 7.3 %all-to-all-start.3 = ((bf16[32,10,1024]{2,1,0:T(8,128)(2,1)}), bf16[32,10,1024]{2,1,0:T(8,128)(2,1)S(1)}, u32[]{:S(2)}, u32[]{:S(2)}) async-start(bf16[32,10,1024]{2,1,0:T(8,128)(2,1)} %reshape_squeeze.7), calls=%async_computation.3 | async-start | bytes 2097152 | tf_op jit(solution)/shard_map/all_to_all | solution.py:325
  189.9 0.1 copy.21
  190.0 0.1 reshape.71
  190.1 0.0 copy-done.9
  190.1 0.0 copy-done.10
  190.1 0.1 copy.19
  190.2 1.2 convert_reduce_fusion.1
  191.5 1.3 reshape.45
  192.8 0.8 gather_fusion.2
  193.6 0.3 reshape.70
  193.9 20.3 %all-to-all-done.3 = bf16[32,10,1024]{2,1,0:T(8,128)(2,1)S(1)} async-done(((bf16[32,10,1024]{2,1,0:T(8,128)(2,1)}), bf16[32,10,1024]{2,1,0:T(8,128)(2,1)S(1)}, u32[]{:S(2)}, u32[]{:S(2)}) %all-to-all-start.3) | async-done | bytes 655392 | tf_op jit(solution)/shard_map/all_to_all | solution.py:325
  214.2 1.2 convert_reduce_fusion
  215.5 1.3 reshape.48
  216.8 0.8 gather_fusion.3
  217.6 0.3 reshape.78
  217.9 1.4 multiply_reduce_fusion
  219.4 0.8 add_convert_fusion
  (12 shorter events, 0.1 us)
Async XLA Ops:
  7.2 131.1 %all-gather.3.cloned.1.call-start = ((), (), s32[]{:S(2)}) async-start(), calls=%async_computation.4 | async-start | bytes 4456448 | tf_op jit(solution)/shard_map/all_gather | solution.py:307
  7.9 136.9 %all-gather.5.cloned.1.call-start = ((), (), s32[]{:S(2)}) async-start(), calls=%async_computation.5 | async-start | bytes 4456448 | tf_op jit(solution)/shard_map/all_gather | solution.py:317
  9.7 0.9 copy-start
  10.6 0.9 copy-start.1
  11.6 0.9 copy-start.2
  12.5 0.9 copy-start.3
  13.4 0.9 copy-start.4
  14.3 0.9 copy-start.5
  15.2 0.9 copy-start.6
  16.1 0.9 copy-start.7
  17.0 0.7 copy-start.8
  67.6 38.3 %all-to-all-start = ((bf16[32,10,1024]{2,1,0:T(8,128)(2,1)}), bf16[32,10,1024]{2,1,0:T(8,128)(2,1)S(1)}, u32[]{:S(2)}, u32[]{:S(2)}) async-start(bf16[32,10,1024]{2,1,0:T(8,128)(2,1)} %bitcast.1), calls=%async_computation | async-start | bytes 2097152 | tf_op jit(solution)/shard_map/all_to_all | solution.py:298
  107.1 30.9 %all-to-all-start.1 = ((bf16[32,10,1024]{2,1,0:T(8,128)(2,1)}), bf16[32,10,1024]{2,1,0:T(8,128)(2,1)S(1)}, u32[]{:S(2)}, u32[]{:S(2)}) async-start(bf16[32,10,1024]{2,1,0:T(8,128)(2,1)} %bitcast.2), calls=%async_computation.1 | async-start | bytes 2097152 | tf_op jit(solution)/shard_map/all_to_all | solution.py:299
  151.2 38.9 %copy-start.9 = (s32[64,2]{0,1:T(2,128)S(1)}, s32[64,2]{0,1:T(2,128)}, u32[]{:S(2)}) copy-start(s32[64,2]{0,1:T(2,128)} %param.25) | copy-start | bytes 1540
  151.2 38.9 %copy-start.10 = (s32[64,2]{0,1:T(2,128)S(1)}, s32[64,2]{0,1:T(2,128)}, u32[]{:S(2)}) copy-start(s32[64,2]{0,1:T(2,128)} %param.24) | copy-start | bytes 1540
  151.2 31.3 %all-to-all-start.2 = ((bf16[32,10,1024]{2,1,0:T(8,128)(2,1)}), bf16[32,10,1024]{2,1,0:T(8,128)(2,1)S(1)}, u32[]{:S(2)}, u32[]{:S(2)}) async-start(bf16[32,10,1024]{2,1,0:T(8,128)(2,1)} %reshape_squeeze.6), calls=%async_computation.2 | async-start | bytes 2097152 | tf_op jit(solution)/shard_map/all_to_all | solution.py:324
  182.5 31.7 %all-to-all-start.3 = ((bf16[32,10,1024]{2,1,0:T(8,128)(2,1)}), bf16[32,10,1024]{2,1,0:T(8,128)(2,1)S(1)}, u32[]{:S(2)}, u32[]{:S(2)}) async-start(bf16[32,10,1024]{2,1,0:T(8,128)(2,1)} %reshape_squeeze.7), calls=%async_computation.3 | async-start | bytes 2097152 | tf_op jit(solution)/shard_map/all_to_all | solution.py:325
Sparse Core Ops, SparseCore 0:
  10.0 74.4 all-gather.2
  86.7 45.4 all-gather.4

commit v2 on v1

v2 whole, which is shorter than its diff:
```python
import functools

import jax
import jax.numpy as jnp
from jax import lax
from jax.experimental import pallas as pl
from jax.experimental.pallas import tpu as pltpu
from jax.sharding import PartitionSpec as P

MESH = pl.DeviceIdType.MESH
HEAD_DIM = 64
BF16 = jnp.bfloat16
F32 = jnp.float32

epsilon = 1e-06
gelu_coef = 0.7978845608028654
cubic_coef = 0.044715


def gelu_pair(inputs, tangent):
    inner_arg = gelu_coef * (inputs + cubic_coef * inputs * inputs * inputs)
    hyperbolic = jnp.tanh(inner_arg)
    values = 0.5 * inputs * (1.0 + hyperbolic)
    slopes = 0.5 * (1.0 + hyperbolic) + 0.5 * inputs * (
        1.0 - hyperbolic * hyperbolic
    ) * gelu_coef * (1.0 + 3.0 * cubic_coef * inputs * inputs)
    return (values, slopes * tangent)


def dot(a, b):
    return jnp.dot(a, b, preferred_element_type=F32)


def one_hot(rows, columns):
    return jnp.where(rows == columns, 1.0, 0.0).astype(BF16)


def iota(shape, dim):
    return lax.broadcasted_iota(jnp.int32, shape, dim)


def ring_order(count):
    order = []
    for j in range(1, count // 2):
        order += [j, count - j]
    return order + [count // 2]


X_SIZE = 4
CHUNK = 256


def front_kernel(
    n,
    y_size,
    capacity,
    q_in,
    k_in,
    v_in,
    dq_in,
    dk_in,
    dv_in,
    stream_in,
    stream_tangent_in,
    gain,
    ids,
    slots,
    state_out,
    tangent_out,
    rows_out,
    fetched,
    fetch_sem,
    x_send,
    yz_send,
    x_all,
    yz_all,
    k_top,
    k_low,
    z_low,
    o_send,
    o_all,
    pick,
    sort,
    tokens,
    message,
    middle,
    landed,
    x_sent,
    x_came,
    yz_sent,
    yz_came,
    o_sent,
    o_came,
    m_sent,
    m_came,
    f_sent,
    f_came,
):
    sources = (q_in, k_in, v_in, dq_in, dk_in, dv_in, stream_in, stream_tangent_in)
    fetches = [
        pltpu.make_async_copy(source, fetched.at[i], fetch_sem.at[i])
        for i, source in enumerate(sources)
    ]
    for copy in fetches:
        copy.start()
    rows, width = stream_in.shape
    me = lax.axis_index("seq")
    place = lax.axis_index("exp")
    my_x, my_y = lax.rem(place, X_SIZE), place // X_SIZE
    barrier = pltpu.get_barrier_semaphore()

    def at_y(y):
        return {"exp": y * X_SIZE + my_x}

    def at_x(x):
        return {"exp": my_y * X_SIZE + x}

    def greet(j, carry):
        pl.semaphore_signal(
            barrier, inc=1, device_id={"seq": lax.rem(me + j, n)}, device_id_type=MESH
        )
        return carry

    lax.fori_loop(1, n, greet, 0)
    for j in range(1, y_size):
        pl.semaphore_signal(
            barrier, inc=1, device_id=at_y(lax.rem(my_y + j, y_size)), device_id_type=MESH
        )
    for j in range(1, X_SIZE):
        pl.semaphore_signal(
            barrier, inc=1, device_id=at_x(lax.rem(my_x + j, X_SIZE)), device_id_type=MESH
        )
    for copy in fetches[:6]:
        copy.wait()
    for h in range(n):
        cols = slice(h * HEAD_DIM, (h + 1) * HEAD_DIM)
        q, k, v, dq, dk, dv = (fetched[i, :, cols] for i in range(6))
        x_send[h] = jnp.concatenate((dq, q), axis=1) * BF16(HEAD_DIM**-0.5)
        yz_send[h] = jnp.concatenate((k, dk, v, dv), axis=1)
    pl.semaphore_wait(barrier, n - 1 + y_size - 1 + X_SIZE - 1)

    def part(index):
        return pl.ds(pl.multiple_of(index * rows, rows), rows)

    def yz_copy(dest, slot):
        return pltpu.make_async_remote_copy(
            src_ref=yz_send.at[dest],
            dst_ref=yz_all.at[part(slot)],
            send_sem=yz_sent.at[dest],
            recv_sem=yz_came.at[slot],
            device_id={"seq": dest},
            device_id_type=MESH,
        )

    def x_copy(dest, slot):
        return pltpu.make_async_remote_copy(
            src_ref=x_send.at[dest],
            dst_ref=x_all.at[part(slot)],
            send_sem=x_sent.at[dest],
            recv_sem=x_came.at[slot],
            device_id={"seq": dest},
            device_id_type=MESH,
        )

    def o_copy(dest, slot):
        return pltpu.make_async_remote_copy(
            src_ref=o_send.at[part(dest)],
            dst_ref=o_all.at[slot],
            send_sem=o_sent.at[dest],
            recv_sem=o_came.at[slot],
            device_id={"seq": dest},
            device_id_type=MESH,
        )

    for make in (yz_copy, x_copy):

        def send(j, carry):
            make(lax.rem(me + j, n), me).start()
            make(lax.rem(me + n - j, n), me).start()
            return carry

        lax.fori_loop(1, n // 2, send, 0)
        make(lax.rem(me + n // 2, n), me).start()

    yz_all[part(me)] = yz_send[me]
    x_all[part(me)] = x_send[me]

    chunks = width // CHUNK
    experts = 2 * y_size
    codes = jnp.where(slots[...] >= 0, ids[...] * capacity + slots[...], -1)
    span_codes = experts * capacity
    wide = []
    for choice in range(2):
        column = jnp.broadcast_to(codes[:, choice : choice + 1].astype(F32), (rows, 128))
        row = column.T[:1].astype(jnp.int32)
        wide.append(
            jnp.concatenate(
                [jnp.where(row >= 0, row + span_codes * i, -1) for i in range(2 * chunks)], axis=1
            )
        )
    depth = 2 * capacity * chunks
    line = iota((depth, 1), 0)
    kind = line // capacity
    wanted = lax.rem(line, capacity) + span_codes * kind

    def choose(expert, carry):
        target = wanted + expert * capacity
        hit = (target == wide[0]) | (target == wide[1])
        pick[pl.ds(pl.multiple_of(expert * depth, depth), depth)] = jnp.where(
            hit, 1.0, 0.0
        ).astype(BF16)
        return carry

    lax.fori_loop(0, experts, choose, 0)
    half = y_size // 2
    size = half * depth
    line = iota((size, 1), 0)
    kind = line // (half * capacity)
    inner = lax.rem(line, half * capacity)
    sort[...] = one_hot(
        (inner // capacity) * depth + kind * capacity + lax.rem(inner, capacity),
        iota((size, size), 1),
    )

    def yz_arrive(j, carry):
        other = lax.rem(me + j, n)
        yz_copy(other, other).wait_recv()
        return carry

    lax.fori_loop(1, n, yz_arrive, 0)
    turned = yz_all[:, : 2 * HEAD_DIM].T
    k_low[...] = turned
    k_top[:HEAD_DIM] = jnp.zeros_like(turned[:HEAD_DIM])
    k_top[HEAD_DIM:] = turned[:HEAD_DIM]
    z_low[...] = jnp.concatenate(
        (
            jnp.zeros((n * rows, HEAD_DIM), BF16),
            yz_all[:, 2 * HEAD_DIM : 3 * HEAD_DIM],
        ),
        axis=1,
    )
    per = 4
    blocks = n // per
    for i in range(blocks):
        block = lax.rem(me // per + i, blocks)
        for u in range(per):
            other = block * per + u

            @pl.when(other != me)
            def _():
                x_copy(other, other).wait_recv()

        span = pl.ds(pl.multiple_of(block * per * rows, per * rows), per * rows)
        x = x_all[span]
        scores = dot(x, k_top[...])
        drift = dot(x, k_low[...])
        weights = jnp.exp(scores - jnp.max(scores, axis=1, keepdims=True))
        weights = weights * (1.0 / jnp.sum(weights, axis=1, keepdims=True))
        drifted = weights * drift
        mean = jnp.sum(drifted, axis=1, keepdims=True)
        both = dot(weights.astype(BF16), yz_all[:, 2 * HEAD_DIM :])
        low = dot(drifted.astype(BF16), z_low[...])
        attended = both[:, :HEAD_DIM]
        moved = low[:, HEAD_DIM:] - mean * attended + both[:, HEAD_DIM:]
        o_send[span] = jnp.concatenate((attended, moved), axis=1).astype(BF16)
        for u in range(per):
            other = block * per + u

            @pl.when(other != me)
            def _():
                o_copy(other, me).start()

    o_all[me] = o_send[part(me)]
    for copy in fetches[6:]:
        copy.wait()

    def o_arrive(j, carry):
        other = lax.rem(me + j, n)
        o_copy(other, other).wait_recv()
        return carry

    lax.fori_loop(1, n, o_arrive, 0)
    for h in range(0, n, 2):
        cols = slice(h * HEAD_DIM, (h + 2) * HEAD_DIM)
        first = o_all[h].astype(F32)
        second = o_all[h + 1].astype(F32)
        state_out[:, cols] = fetched[6, :, cols].astype(F32) + jnp.concatenate(
            (first[:, :HEAD_DIM], second[:, :HEAD_DIM]), axis=1
        )
        tangent_out[:, cols] = fetched[7, :, cols].astype(F32) + jnp.concatenate(
            (first[:, HEAD_DIM:], second[:, HEAD_DIM:]), axis=1
        )
    state = state_out[...]
    tangent = tangent_out[...]
    inverse = lax.rsqrt(jnp.mean(state * state, axis=1, keepdims=True) + epsilon)
    cross = jnp.mean(state * tangent, axis=1, keepdims=True)
    normed = (gain[...] * state * inverse).astype(BF16)
    normed_tangent = (
        gain[...] * inverse * (tangent - state * cross * inverse * inverse)
    ).astype(BF16)
    for c in range(chunks):
        cols = slice(c * CHUNK, (c + 1) * CHUNK)
        tokens[2 * c * rows : (2 * c + 1) * rows] = normed[:, cols]
        tokens[(2 * c + 1) * rows : (2 * c + 2) * rows] = normed_tangent[:, cols]

    def m_copy(dest, slot):
        return pltpu.make_async_remote_copy(
            src_ref=message.at[dest],
            dst_ref=middle.at[slot],
            send_sem=m_sent.at[dest],
            recv_sem=m_came.at[slot],
            device_id=at_y(dest),
            device_id_type=MESH,
        )

    def f_copy(dest, source_x, source_y):
        pair = pl.ds(pl.multiple_of((dest // 2) * depth, depth), depth)
        return pltpu.make_async_remote_copy(
            src_ref=middle.at[source_y, pair],
            dst_ref=landed.at[source_x, source_y],
            send_sem=f_sent.at[dest, source_y],
            recv_sem=f_came.at[source_x, source_y],
            device_id=at_x(dest),
            device_id_type=MESH,
        )

    def fill(dest):
        picked = pick[pl.ds(pl.multiple_of(dest * 2 * depth, 2 * depth), 2 * depth)]
        return dot(picked, tokens[...]).astype(BF16)

    def spread(source_y):
        for j in (1, 3, 2):
            f_copy(lax.rem(my_x + j, X_SIZE), my_x, source_y).start()
        landed[my_x, source_y] = middle[
            source_y, pl.ds(pl.multiple_of((my_x // 2) * depth, depth), depth)
        ]

    order = ring_order(y_size)
    for j in order:
        dest = lax.rem(my_y + j, y_size)
        message[dest] = fill(dest)
        m_copy(dest, my_y).start()
    middle[my_y] = fill(my_y)
    spread(my_y)
    for j in order:
        other = lax.rem(my_y + j, y_size)
        m_copy(other, other).wait_recv()
        spread(other)
    for j in [0] + order:
        other = lax.rem(my_y + j, y_size)
        for i in range(1, X_SIZE):
            source = lax.rem(my_x + i, X_SIZE)
            f_copy(source, source, other).wait_recv()
    group = half * capacity
    for x in range(X_SIZE):
        sorted_rows = [
            dot(sort[...], landed[x, side * half : (side + 1) * half].reshape(size, CHUNK))
            for side in range(2)
        ]
        for c in range(chunks):
            for tangent_kind in range(2):
                top = (2 * c + tangent_kind) * group
                rows_out[
                    pl.ds((tangent_kind * X_SIZE + x) * 2 * group, 2 * group),
                    pl.ds(c * CHUNK, CHUNK),
                ] = jnp.concatenate(
                    [values[top : top + group] for values in sorted_rows], axis=0
                ).astype(BF16)

    def drain(j, carry):
        other = lax.rem(me + j, n)
        yz_copy(other, me).wait_send()
        x_copy(other, me).wait_send()
        o_copy(other, me).wait_send()
        return carry

    lax.fori_loop(1, n, drain, 0)
    for j in order:
        m_copy(lax.rem(my_y + j, y_size), my_y).wait_send()
    for y in range(y_size):
        for j in range(1, X_SIZE):
            f_copy(lax.rem(my_x + j, X_SIZE), my_x, y).wait_send()


def front(arrays, gain, ids, slots, capacity):
    n = lax.axis_size("seq")
    y_size = lax.axis_size("exp") // X_SIZE
    rows, width = arrays[0].shape
    total = n * rows
    chunks = width // CHUNK
    depth = 2 * capacity * chunks
    vmem = pl.BlockSpec(memory_space=pltpu.VMEM)
    away = pl.BlockSpec(memory_space=pl.ANY)
    dma = pltpu.SemaphoreType.DMA
    return pl.pallas_call(
        functools.partial(front_kernel, n, y_size, capacity),
        out_shape=(
            jax.ShapeDtypeStruct((rows, width), F32),
            jax.ShapeDtypeStruct((rows, width), F32),
            jax.ShapeDtypeStruct((2 * X_SIZE * y_size * capacity, width), BF16),
        ),
        in_specs=[away] * 8 + [vmem] * 3,
        out_specs=(vmem,) * 3,
        scratch_shapes=[
            pltpu.VMEM((8, rows, width), BF16),
            dma((8,)),
            pltpu.VMEM((n, rows, 2 * HEAD_DIM), BF16),
            pltpu.VMEM((n, rows, 4 * HEAD_DIM), BF16),
            pltpu.VMEM((total, 2 * HEAD_DIM), BF16),
            pltpu.VMEM((total, 4 * HEAD_DIM), BF16),
            pltpu.VMEM((2 * HEAD_DIM, total), BF16),
            pltpu.VMEM((2 * HEAD_DIM, total), BF16),
            pltpu.VMEM((total, 2 * HEAD_DIM), BF16),
            pltpu.VMEM((total, 2 * HEAD_DIM), BF16),
            pltpu.VMEM((n, rows, 2 * HEAD_DIM), BF16),
            pltpu.VMEM((2 * y_size * depth, 2 * chunks * rows), BF16),
            pltpu.VMEM((y_size // 2 * depth, y_size // 2 * depth), BF16),
            pltpu.VMEM((2 * chunks * rows, CHUNK), BF16),
            pltpu.VMEM((y_size, 2 * depth, CHUNK), BF16),
            pltpu.VMEM((y_size, 2 * depth, CHUNK), BF16),
            pltpu.VMEM((X_SIZE, y_size, depth, CHUNK), BF16),
        ]
        + [dma((n,))] * 6
        + [dma((y_size,))] * 2
        + [dma((X_SIZE, y_size))] * 2,
        compiler_params=pltpu.CompilerParams(
            collective_id=0, has_side_effects=True, vmem_limit_bytes=48 * 1024 * 1024
        ),
        name="front",
    )(*arrays, gain.reshape(1, width), ids, slots)


def back_kernel(
    n,
    y_size,
    capacity,
    rows_in,
    first_in,
    second_in,
    state,
    tangent,
    ids,
    gates,
    slots,
    out,
    out_tangent,
    first,
    second,
    active,
    sort,
    gate_high,
    gate_low,
    halves_send,
    halves,
    sums_send,
    sums,
    a_own,
    a_sent,
    a_came,
    b_own,
    b_sent,
    b_came,
    h_sent,
    h_came,
    s_sent,
    s_came,
):
    me = lax.axis_index("seq")
    core = lax.rem(me, 2)
    partner = me + 1 - 2 * core
    place = lax.axis_index("exp")
    my_x, my_y = lax.rem(place, X_SIZE), place // X_SIZE
    tokens, width = state.shape
    chunks = width // CHUNK
    shards, _, units = first_in.shape
    barrier = pltpu.get_barrier_semaphore()

    def at_y(y):
        return {"exp": y * X_SIZE + my_x}

    def at_x(x):
        return {"exp": my_y * X_SIZE + x}

    pl.semaphore_signal(barrier, inc=1, device_id={"seq": partner}, device_id_type=MESH)
    for j in range(1, X_SIZE):
        pl.semaphore_signal(
            barrier, inc=1, device_id=at_x(lax.rem(my_x + j, X_SIZE)), device_id_type=MESH
        )
    for j in range(1, y_size):
        pl.semaphore_signal(
            barrier, inc=1, device_id=at_y(lax.rem(my_y + j, y_size)), device_id_type=MESH
        )

    def first_own(j):
        return pltpu.make_async_copy(first_in.at[j], first.at[2 * j + core], a_own.at[j])

    def first_copy(j, owner):
        return pltpu.make_async_remote_copy(
            src_ref=first_in.at[j],
            dst_ref=first.at[2 * j + owner],
            send_sem=a_sent.at[j],
            recv_sem=a_came.at[j],
            device_id={"seq": partner},
            device_id_type=MESH,
        )

    def second_part(j, owner):
        return second.at[pl.ds(pl.multiple_of((2 * j + owner) * units, units), units)]

    def second_own(j):
        return pltpu.make_async_copy(second_in.at[j], second_part(j, core), b_own.at[j])

    def second_copy(j, owner):
        return pltpu.make_async_remote_copy(
            src_ref=second_in.at[j],
            dst_ref=second_part(j, owner),
            send_sem=b_sent.at[j],
            recv_sem=b_came.at[j],
            device_id={"seq": partner},
            device_id_type=MESH,
        )

    for j in range(shards):
        first_own(j).start()
    for j in range(shards):
        second_own(j).start()
    pl.semaphore_wait(barrier, 1 + X_SIZE - 1 + y_size - 1)
    for j in range(shards):
        first_copy(j, core).start()
    for j in range(shards):
        second_copy(j, core).start()

    experts = 2 * y_size
    span_codes = experts * capacity
    parts = CHUNK // 128
    depth = parts * 2 * capacity
    line = iota((1, experts * depth), 1)
    inner = lax.rem(line, depth)
    column_codes = (
        (line // depth) * capacity + lax.rem(inner, capacity) + span_codes * (inner // capacity)
    )
    high = jnp.zeros((2 * parts * tokens, experts * depth), F32)
    low = high
    for choice in range(2):
        pick = slice(choice, choice + 1)
        slot = slots[:, pick]
        code = jnp.where(slot >= 0, ids[:, pick] * capacity + slot, -1)
        code = jnp.concatenate(
            [jnp.where(code >= 0, code + span_codes * i, -1) for i in range(2 * parts)], axis=0
        )
        top = gates[:, pick] // 256
        rest = gates[:, pick] - top * 256
        top = jnp.concatenate([top.astype(F32)] * (2 * parts), axis=0)
        rest = jnp.concatenate([rest.astype(F32)] * (2 * parts), axis=0)
        hit = code == column_codes
        high = high + jnp.where(hit, top, 0.0)
        low = low + jnp.where(hit, rest, 0.0)
    gate_high[...] = high.astype(BF16)
    gate_low[...] = low.astype(BF16)
    size = parts * 2 * y_size * capacity
    line = iota((size, 1), 0)
    inner = lax.rem(line, depth)
    sort[...] = one_hot(
        (inner // capacity) * (y_size * capacity)
        + (line // depth) * capacity
        + lax.rem(inner, capacity),
        iota((size, size), 1),
    )

    count = rows_in.shape[0] // 2

    def project(j, carry):
        first_own(j).wait()
        first_copy(j, 1 - core).wait_recv()
        weights = jnp.concatenate((first[2 * j], first[2 * j + 1]), axis=1)
        hidden = dot(rows_in[...], weights)
        values, slopes = gelu_pair(hidden[:count], hidden[count:])
        cols = pl.ds(pl.multiple_of(j * 2 * units, 2 * units), 2 * units)
        active[:count, cols] = values.astype(BF16)
        active[count:, cols] = slopes.astype(BF16)
        return carry

    lax.fori_loop(0, shards, project, 0)

    def second_wait(j, carry):
        second_own(j).wait()
        second_copy(j, 1 - core).wait_recv()
        return carry

    lax.fori_loop(0, shards, second_wait, 0)

    block = y_size * capacity

    def h_copy(c, dest, slot):
        return pltpu.make_async_remote_copy(
            src_ref=halves_send.at[c, dest],
            dst_ref=halves.at[c, slot],
            send_sem=h_sent.at[c, dest],
            recv_sem=h_came.at[c, slot],
            device_id=at_x(dest),
            device_id_type=MESH,
        )

    def s_copy(c, dest, slot):
        return pltpu.make_async_remote_copy(
            src_ref=sums_send.at[c, dest],
            dst_ref=sums.at[c, slot],
            send_sem=s_sent.at[c, dest],
            recv_sem=s_came.at[c, slot],
            device_id=at_y(dest),
            device_id_type=MESH,
        )

    order = ring_order(y_size)

    def expert_block(c):
        done = dot(active[...], second[:, c * CHUNK : (c + 1) * CHUNK]).astype(BF16)
        for x in range(X_SIZE):
            halves_send[c, x, :block] = done[x * block : (x + 1) * block]
            halves_send[c, x, block:] = done[count + x * block : count + (x + 1) * block]
        for j in (1, 3, 2):
            h_copy(c, lax.rem(my_x + j, X_SIZE), my_x).start()
        halves[c, my_x] = halves_send[c, my_x]

    def return_block(c):
        for j in (1, 3, 2):
            source = lax.rem(my_x + j, X_SIZE)
            h_copy(c, source, source).wait_recv()
        pair = [
            (halves[c, 2 * p].astype(F32) + halves[c, 2 * p + 1].astype(F32)).astype(BF16)
            for p in range(2)
        ]
        stacked = jnp.concatenate(
            [
                jnp.concatenate([total[:, i * 128 : (i + 1) * 128] for total in pair], axis=1)
                for i in range(parts)
            ],
            axis=0,
        )
        ready = dot(sort[...], stacked)
        for y in range(y_size):
            piece = ready[y * depth : (y + 1) * depth]
            sums_send[c, y] = jnp.concatenate((piece[:, :128], piece[:, 128:]), axis=0).astype(
                BF16
            )
        for j in order:
            s_copy(c, lax.rem(my_y + j, y_size), my_y).start()
        sums[c, my_y] = sums_send[c, my_y]

    def mix_block(c):
        for j in order:
            source = lax.rem(my_y + j, y_size)
            s_copy(c, source, source).wait_recv()
        values = sums[c].reshape(experts * depth, 128)
        mixed = (dot(gate_high[...], values) * 256.0 + dot(gate_low[...], values)) * (
            1.0 / 65536.0
        )
        for i in range(parts):
            cols = slice(c * CHUNK + i * 128, c * CHUNK + (i + 1) * 128)
            top = 2 * i * tokens
            out[:, cols] = (state[:, cols] + mixed[top : top + tokens]).astype(BF16)
            out_tangent[:, cols] = (
                tangent[:, cols] + mixed[top + tokens : top + 2 * tokens]
            ).astype(BF16)

    for c in range(chunks):
        expert_block(c)
        if c:
            return_block(c - 1)
    return_block(chunks - 1)
    for c in range(chunks):
        mix_block(c)

    def drain(j, carry):
        first_copy(j, core).wait_send()
        second_copy(j, core).wait_send()
        return carry

    lax.fori_loop(0, shards, drain, 0)
    for c in range(chunks):
        for j in range(1, X_SIZE):
            h_copy(c, lax.rem(my_x + j, X_SIZE), my_x).wait_send()
        for j in order:
            s_copy(c, lax.rem(my_y + j, y_size), my_y).wait_send()


def back(rows_in, first_in, second_in, state, tangent, ids, gates, slots, capacity):
    n = lax.axis_size("seq")
    y_size = lax.axis_size("exp") // X_SIZE
    tokens, width = state.shape
    chunks = width // CHUNK
    shards, _, units = first_in.shape
    parts = CHUNK // 128
    depth = parts * 2 * capacity
    block = y_size * capacity
    size = parts * 2 * block
    vmem = pl.BlockSpec(memory_space=pltpu.VMEM)
    away = pl.BlockSpec(memory_space=pl.ANY)
    dma = pltpu.SemaphoreType.DMA
    return pl.pallas_call(
        functools.partial(back_kernel, n, y_size, capacity),
        out_shape=(
            jax.ShapeDtypeStruct((tokens, width), BF16),
            jax.ShapeDtypeStruct((tokens, width), BF16),
        ),
        in_specs=[vmem, away, away] + [vmem] * 5,
        out_specs=(vmem,) * 2,
        scratch_shapes=[
            pltpu.VMEM((2 * shards, width, units), BF16),
            pltpu.VMEM((2 * shards * units, width), BF16),
            pltpu.VMEM((2 * X_SIZE * block, 2 * shards * units), BF16),
            pltpu.VMEM((size, size), BF16),
            pltpu.VMEM((2 * parts * tokens, 2 * y_size * depth), BF16),
            pltpu.VMEM((2 * parts * tokens, 2 * y_size * depth), BF16),
            pltpu.VMEM((chunks, X_SIZE, 2 * block, CHUNK), BF16),
            pltpu.VMEM((chunks, X_SIZE, 2 * block, CHUNK), BF16),
            pltpu.VMEM((chunks, y_size, 2 * depth, 128), BF16),
            pltpu.VMEM((chunks, y_size, 2 * depth, 128), BF16),
        ]
        + [dma((shards,))] * 6
        + [dma((chunks, X_SIZE))] * 2
        + [dma((chunks, y_size))] * 2,
        compiler_params=pltpu.CompilerParams(
            collective_id=1, has_side_effects=True, vmem_limit_bytes=48 * 1024 * 1024
        ),
        name="back",
    )(rows_in, first_in, second_in, state, tangent, ids, gates, slots)


def per_device(
    query_rows,
    key_rows,
    value_rows,
    query_tangent,
    key_tangent,
    value_tangent,
    stream,
    stream_tangent,
    norm_gain,
    expert_ids,
    gate_units,
    slot_index,
    weight_in,
    weight_out,
):
    n = lax.axis_size("seq")
    expert_count = lax.axis_size("exp") // 2
    local_rows = stream.shape[0]
    capacity = 2 * ((5 * local_rows + 4 * expert_count - 1) // (4 * expert_count))
    same_core = [list(range(core, n, 2)) for core in range(2)]
    first = lax.all_gather(weight_in, "seq", axis_index_groups=same_core)
    second = lax.all_gather(weight_out, "seq", axis_index_groups=same_core)
    state, tangent, rows = front(
        (
            query_rows,
            key_rows,
            value_rows,
            query_tangent,
            key_tangent,
            value_tangent,
            stream,
            stream_tangent,
        ),
        norm_gain,
        expert_ids,
        slot_index,
        capacity,
    )
    return back(
        rows, first, second, state, tangent, expert_ids, gate_units, slot_index, capacity
    )


def solution(mesh):
    rows = P(("exp", "seq"), None)
    return jax.shard_map(
        per_device,
        mesh=mesh,
        in_specs=(rows,) * 8 + (P(),) + (rows,) * 3 + (P(None, ("exp", "seq")), rows),
        out_specs=(rows, rows),
        check_vma=False,
    )
```

time: 231 us -> 174 us (0.75); the launches traced: 227 us -> 174 us
  Pallas kernels: 46.6 us -> 124 us
  waiting for transfers between devices: 97.7 us -> 23.1 us
  starting transfers between devices: 29.5 us -> 0.08 us
  matrix products: 9.73 us -> 0 us
  local copies, waits for them, and re-layouts: 21.9 us -> 13.1 us
  other arithmetic: 7.23 us -> 0 us
    all_to_all x4 -> x0, waiting for transfers between devices: 96.2 us -> none  [the longest x1 27.1 us: per_device(): lax.all_to_all(outgoing, 'exp', split_axis=0, concat_axis=0, tiled=True)]
    pallas_call x1 -> x2, Pallas kernels: 46.6 us -> 124 us  [the longest x1 78.9 us: front(): pl.pallas_call(functools.partial(front_kernel, n, y_size, capacity), out_...]
    all_to_all x4 -> x0, starting transfers between devices: 29.5 us -> none  [the longest x1 10.1 us: per_device(): lax.all_to_all(outgoing, 'exp', split_axis=0, concat_axis=0, tiled=True)]
    all_gather x2, waiting for transfers between devices: 0.04 us -> 21.7 us  [the longest x1 21.7 us: per_device(): second = lax.all_gather(weight_out, 'seq', axis_index_groups=same_core)]
    dot_general x2 -> x0, matrix products: 9.73 us -> none  [the longest x1 5.05 us: per_device(): jnp.einsum('prn,nd->prd', activated_pair, lax.all_gather(weight_out, 'seq...]
    unnamed x22 -> x25, local copies, waits for them, and re-layouts: 7.92 us -> 13.1 us
    gather x6 -> x0, local copies, waits for them, and re-layouts: 4.1 us -> none  [the longest x2 1.11 us: per_device(): expert_sums[flat_index]]
    reduce_sum x3 -> x0, other arithmetic: 3.9 us -> none  [the longest x1 1.45 us: per_device(): jnp.sum(gate_values[:, :, None] * expert_drifts[flat_index], axis=1)]
  transfers between devices with their start and end apart: 6 -> 2, of which waited for: 4 -> 1; matrix products, arithmetic and copies ran while one was open for 8% -> 1% of each run, Pallas kernels for 21% -> 45%
where the time goes in v2:
time: 174 us
  Pallas kernels  124 us (71%)
  waiting for transfers between devices  23.1 us (13%)
  between operations  14.1 us (8%)
  local copies, waits for them, and re-layouts  13.1 us (8%)
    pallas_call x1, Pallas kernels, front(): pl.pallas_call(functools.partial(front_kernel, n, y_size, capacity), out_...  78.9 us
    pallas_call x1, Pallas kernels, back(): pl.pallas_call(functools.partial(back_kernel, n, y_size, capacity), out_s...  44.8 us
    all_gather x1, waiting for transfers between devices, per_device(): second = lax.all_gather(weight_out, 'seq', axis_index_groups=same_core)  21.7 us
    unnamed x25, local copies, waits for them, and re-layouts  13.1 us
  transfers between devices with their start and end apart: 2, of which 1 were waited for; matrix products, arithmetic and copies ran while one was open for 1% of the time, Pallas kernels for 45%

profile of v2, /device:TPU:1, one launch (start us, length us, event | category | flops | bytes accessed | tf_op | source)
XLA Modules:
  0.0 174.0 jit_solution(7710830662835547790)
XLA Ops:
  7.2 0.0 all-gather.5.cloned.1.call-start
  7.2 0.7 all-gather.5.cloned.1.call-update
  7.9 0.0 all-gather.7.cloned.1.call-start
  7.9 0.7 all-gather.7.cloned.1.call-update
  8.6 0.8 copy.16.ids
  9.4 0.8 copy.17.slots
  10.2 0.8 copy.19.gates
  11.0 0.0 copy-start.1
  11.0 0.9 copy-done.1
  11.9 0.0 copy-start.2
  11.9 0.9 copy-done.2
  12.8 0.0 copy-start.3
  12.8 0.9 copy-done.3
  13.7 0.0 copy-start.4
  13.7 0.9 copy-done.4
  14.6 0.0 copy-start.5
  14.6 0.9 copy-done.5
  15.5 0.0 copy-start.6
  15.5 0.9 copy-done.6
  16.4 0.0 copy-start.7
  16.4 0.9 copy-done.7
  17.3 0.0 copy-start.8
  17.3 0.9 copy-done.8
  18.2 0.0 copy-start.9
  18.2 0.7 copy-done.9
  18.9 78.9 %front.1 = (f32[64,1024]{1,0:T(8,128)S(1)}, f32[64,1024]{1,0:T(8,128)S(1)}, bf16[640,1024]{1,0:T(8,128)(2,1)S(1)}) custom-call(bf16[64,1024]{1,0:T(8,128)(2,1)S(1)} %copy-done.1, bf16[64,1024]{1,0:T(8,128)(2,1)S(1)} %copy-done.2, bf16[64,1024]{1,0:T(8,128)(2,1)S(1)} %copy-done.3, bf16[64,1024]{1,0:T(8,128)(2,1)S(1)} %copy-done.4, ...), custom_call_target="tpu_custom_call" | custom-call | tf_op jit(solution)/shard_map/front/pallas_call | solution.py:395
  97.8 0.0 all-gather.5.cloned.1.call-done
  97.8 21.7 %all-gather.7.cloned.1.call-done = bf16[1024,1024]{1,0:T(8,128)(2,1)} async-done(((bf16[128,1024]{1,0:T(8,128)(2,1)}), bf16[1024,1024]{1,0:T(8,128)(2,1)}) %all-gather.7.cloned.1.call-update) | async-done | bytes 2097168 | tf_op jit(solution)/shard_map/all_gather | solution.py:752
  119.5 0.0 copy-start
  119.5 1.6 copy-done
  121.1 44.8 %back.1 = (bf16[64,1024]{1,0:T(8,128)(2,1)S(1)}, bf16[64,1024]{1,0:T(8,128)(2,1)S(1)}) custom-call(bf16[640,1024]{1,0:T(8,128)(2,1)S(1)} %get-tuple-element.5.rows_in, bf16[8,1024,128]{2,1,0:T(8,128)(2,1)S(1)} %bitcast.3, bf16[8,128,1024]{2,1,0:T(8,128)(2,1)} %bitcast.5, f32[64,1024]{1,0:T(8,128)S(1)} %get-tuple-element.6.state, ...), custom_call_target="tpu_custom_call" | custom-call | tf_op jit(solution)/shard_map/back/pallas_call | solution.py:700
  165.8 0.7 copy.23
  166.5 0.7 copy.24
Async XLA Ops:
  7.2 90.6 %all-gather.5.cloned.1.call-start = ((), (), s32[]{:S(2)}) async-start(), calls=%async_computation | async-start | bytes 2359296 | tf_op jit(solution)/shard_map/all_gather | solution.py:751
  7.9 111.6 %all-gather.7.cloned.1.call-start = ((), (), s32[]{:S(2)}) async-start(), calls=%async_computation.1 | async-start | bytes 2359296 | tf_op jit(solution)/shard_map/all_gather | solution.py:752
  11.0 0.9 copy-start.1
  11.9 0.9 copy-start.2
  12.8 0.9 copy-start.3
  13.7 0.9 copy-start.4
  14.6 0.9 copy-start.5
  15.5 0.9 copy-start.6
  16.4 0.9 copy-start.7
  17.3 0.9 copy-start.8
  18.2 0.7 copy-start.9
  119.5 1.6 copy-start
Sparse Core Ops, SparseCore 0:
  10.1 67.6 all-gather.4
  79.8 39.5 all-gather.6

commit v3 on v1

v3 whole, which is shorter than its diff:
```python
import functools

import jax
import jax.numpy as jnp
from jax import lax
from jax.experimental import pallas as pl
from jax.experimental.pallas import tpu as pltpu
from jax.sharding import PartitionSpec as P

MESH = pl.DeviceIdType.MESH
HEAD_DIM = 64
BF16 = jnp.bfloat16
F32 = jnp.float32

epsilon = 1e-06
gelu_coef = 0.7978845608028654
cubic_coef = 0.044715


def gelu_pair(inputs, tangent):
    inner_arg = gelu_coef * (inputs + cubic_coef * inputs * inputs * inputs)
    hyperbolic = jnp.tanh(inner_arg)
    values = 0.5 * inputs * (1.0 + hyperbolic)
    slopes = 0.5 * (1.0 + hyperbolic) + 0.5 * inputs * (
        1.0 - hyperbolic * hyperbolic
    ) * gelu_coef * (1.0 + 3.0 * cubic_coef * inputs * inputs)
    return (values, slopes * tangent)


def dot(a, b):
    return jnp.dot(a, b, preferred_element_type=F32)


def one_hot(rows, columns):
    return jnp.where(rows == columns, 1.0, 0.0).astype(BF16)


def iota(shape, dim):
    return lax.broadcasted_iota(jnp.int32, shape, dim)


def ring_order(count):
    order = []
    for j in range(1, count // 2):
        order += [j, count - j]
    return order + [count // 2]


X_SIZE = 4
CHUNK = 256


RING_PIECES = 6
HOPS = 4


def block_kernel(
    n,
    y_size,
    capacity,
    q_in,
    k_in,
    v_in,
    dq_in,
    dk_in,
    dv_in,
    stream_in,
    stream_tangent_in,
    gain_in,
    ids_in,
    gates_in,
    slots_in,
    first_in,
    second_in,
    out,
    out_tangent,
    fetched,
    gain,
    numbers,
    first,
    second,
    x_send,
    yz_send,
    x_all,
    yz_all,
    k_top,
    k_low,
    z_low,
    o_send,
    o_all,
    pick,
    sort,
    tokens,
    message,
    middle,
    landed,
    state,
    tangent,
    expert_rows,
    active,
    back_sort,
    gate_high,
    gate_low,
    halves_send,
    halves,
    sums_send,
    sums,
    fetch_sem,
    x_sent,
    x_came,
    yz_sent,
    yz_came,
    o_sent,
    o_came,
    m_sent,
    m_came,
    f_sent,
    f_came,
    w_sent,
    w_came,
    p_sent,
    p_came,
    h_sent,
    h_came,
    s_sent,
    s_came,
):
    rows, width = stream_in.shape
    units = first_in.shape[1]
    me = lax.axis_index("seq")
    core = lax.rem(me, 2)
    partner = me + 1 - 2 * core
    my_z = me // 2
    shards = n // 2
    place = lax.axis_index("exp")
    my_x, my_y = lax.rem(place, X_SIZE), place // X_SIZE
    chunks = width // CHUNK
    experts = 2 * y_size
    span_codes = experts * capacity
    order = ring_order(y_size)

    def at_y(y):
        return {"exp": y * X_SIZE + my_x}

    def at_x(x):
        return {"exp": my_y * X_SIZE + x}

    def part(index):
        return pl.ds(pl.multiple_of(index * rows, rows), rows)

    def unit_rows(index):
        return pl.ds(pl.multiple_of(index * units, units), units)

    sources = (q_in, k_in, v_in, dq_in, dk_in, dv_in, stream_in, stream_tangent_in)
    targets = [fetched.at[i] for i in range(8)]
    sources += (gain_in, ids_in, gates_in, slots_in, first_in, second_in)
    targets += [gain, numbers.at[0], numbers.at[1], numbers.at[2]]
    targets += [first.at[me], second.at[unit_rows(me)]]
    fetches = [
        pltpu.make_async_copy(source, target, fetch_sem.at[i])
        for i, (source, target) in enumerate(zip(sources, targets))
    ]
    for copy in fetches:
        copy.start()

    barrier = pltpu.get_barrier_semaphore()

    def greet(j, carry):
        pl.semaphore_signal(
            barrier, inc=1, device_id={"seq": lax.rem(me + j, n)}, device_id_type=MESH
        )
        return carry

    lax.fori_loop(1, n, greet, 0)
    for j in range(1, y_size):
        pl.semaphore_signal(
            barrier, inc=1, device_id=at_y(lax.rem(my_y + j, y_size)), device_id_type=MESH
        )
    for j in range(1, X_SIZE):
        pl.semaphore_signal(
            barrier, inc=1, device_id=at_x(lax.rem(my_x + j, X_SIZE)), device_id_type=MESH
        )

    def piece_at(piece, index):
        if piece < 2:
            return first.at[index, piece * (width // 2) : (piece + 1) * (width // 2)]
        cols = slice((piece - 2) * CHUNK, (piece - 1) * CHUNK)
        return second.at[unit_rows(index), cols]

    def hops(piece, way):
        return HOPS if (piece + way) % 2 == 0 else HOPS - 1

    def ring_copy(piece, way, hop, arriving):
        step = 1 if way == 0 else shards - 1
        back = hop if arriving else hop - 1
        origin = lax.rem(my_z + (shards - step) * back, shards)
        block = piece_at(piece, 2 * origin + core)
        return pltpu.make_async_remote_copy(
            src_ref=block,
            dst_ref=block,
            send_sem=w_sent.at[piece, way * HOPS + hop - 1],
            recv_sem=w_came.at[piece, way * HOPS + hop - 1],
            device_id={"seq": 2 * lax.rem(my_z + step, shards) + core},
            device_id_type=MESH,
        )

    def share_copy(piece, z, owner):
        block = piece_at(piece, 2 * z + owner)
        return pltpu.make_async_remote_copy(
            src_ref=block,
            dst_ref=block,
            send_sem=p_sent.at[piece, z],
            recv_sem=p_came.at[piece, z],
            device_id={"seq": partner},
            device_id_type=MESH,
        )

    def ring_open(piece):
        for way in range(2):
            ring_copy(piece, way, 1, False).start()
        share_copy(piece, my_z, core).start()

    def ring_step(piece, hop):
        for way in range(2):
            if hop <= hops(piece, way):
                ring_copy(piece, way, hop, True).wait_recv()
                if hop < hops(piece, way):
                    ring_copy(piece, way, hop + 1, False).start()
                step = 1 if way == 0 else shards - 1
                origin = lax.rem(my_z + (shards - step) * hop, shards)
                share_copy(piece, origin, core).start()

    for copy in fetches[:6]:
        copy.wait()
    for h in range(n):
        cols = slice(h * HEAD_DIM, (h + 1) * HEAD_DIM)
        q, k, v, dq, dk, dv = (fetched[i, :, cols] for i in range(6))
        x_send[h] = jnp.concatenate((dq, q), axis=1) * BF16(HEAD_DIM**-0.5)
        yz_send[h] = jnp.concatenate((k, dk, v, dv), axis=1)
    pl.semaphore_wait(barrier, n - 1 + y_size - 1 + X_SIZE - 1)

    def yz_copy(dest, slot):
        return pltpu.make_async_remote_copy(
            src_ref=yz_send.at[dest],
            dst_ref=yz_all.at[part(slot)],
            send_sem=yz_sent.at[dest],
            recv_sem=yz_came.at[slot],
            device_id={"seq": dest},
            device_id_type=MESH,
        )

    def x_copy(dest, slot):
        return pltpu.make_async_remote_copy(
            src_ref=x_send.at[dest],
            dst_ref=x_all.at[part(slot)],
            send_sem=x_sent.at[dest],
            recv_sem=x_came.at[slot],
            device_id={"seq": dest},
            device_id_type=MESH,
        )

    def o_copy(dest, slot):
        return pltpu.make_async_remote_copy(
            src_ref=o_send.at[part(dest)],
            dst_ref=o_all.at[slot],
            send_sem=o_sent.at[dest],
            recv_sem=o_came.at[slot],
            device_id={"seq": dest},
            device_id_type=MESH,
        )

    for make in (yz_copy, x_copy):

        def send(j, carry):
            make(lax.rem(me + j, n), me).start()
            make(lax.rem(me + n - j, n), me).start()
            return carry

        lax.fori_loop(1, n // 2, send, 0)
        make(lax.rem(me + n // 2, n), me).start()

    yz_all[part(me)] = yz_send[me]
    x_all[part(me)] = x_send[me]
    for copy in fetches[6:]:
        copy.wait()

    codes = jnp.where(numbers[2] >= 0, numbers[0] * capacity + numbers[2], -1)
    wide = [
        jnp.concatenate(
            [jnp.where(row >= 0, row + span_codes * i, -1) for i in range(2 * chunks)], axis=1
        )
        for row in (codes[:1], codes[1:])
    ]
    depth = 2 * capacity * chunks
    line = iota((depth, 1), 0)
    wanted = lax.rem(line, capacity) + span_codes * (line // capacity)

    def choose(expert, carry):
        target = wanted + expert * capacity
        hit = (target == wide[0]) | (target == wide[1])
        pick[pl.ds(pl.multiple_of(expert * depth, depth), depth)] = jnp.where(
            hit, 1.0, 0.0
        ).astype(BF16)
        return carry

    lax.fori_loop(0, experts, choose, 0)
    half = y_size // 2
    size = half * depth
    line = iota((size, 1), 0)
    inner = lax.rem(line, half * capacity)
    sort[...] = one_hot(
        (inner // capacity) * depth
        + (line // (half * capacity)) * capacity
        + lax.rem(inner, capacity),
        iota((size, size), 1),
    )

    parts = CHUNK // 128
    back_depth = parts * 2 * capacity
    line = iota((1, experts * back_depth), 1)
    inner = lax.rem(line, back_depth)
    column_codes = (
        (line // back_depth) * capacity
        + lax.rem(inner, capacity)
        + span_codes * (inner // capacity)
    )

    def upright(row):
        return jnp.broadcast_to(row.astype(F32), (128, rows)).T[:, :1].astype(jnp.int32)

    high = jnp.zeros((2 * parts * rows, experts * back_depth), F32)
    low = high
    for choice in range(2):
        code = upright(codes[choice : choice + 1])
        gate = upright(numbers[1, choice : choice + 1])
        code = jnp.concatenate(
            [jnp.where(code >= 0, code + span_codes * i, -1) for i in range(2 * parts)], axis=0
        )
        top = gate // 256
        rest = gate - top * 256
        top = jnp.concatenate([top.astype(F32)] * (2 * parts), axis=0)
        rest = jnp.concatenate([rest.astype(F32)] * (2 * parts), axis=0)
        hit = code == column_codes
        high = high + jnp.where(hit, top, 0.0)
        low = low + jnp.where(hit, rest, 0.0)
    gate_high[...] = high.astype(BF16)
    gate_low[...] = low.astype(BF16)
    back_size = parts * 2 * y_size * capacity
    line = iota((back_size, 1), 0)
    inner = lax.rem(line, back_depth)
    back_sort[...] = one_hot(
        (inner // capacity) * (y_size * capacity)
        + (line // back_depth) * capacity
        + lax.rem(inner, capacity),
        iota((back_size, back_size), 1),
    )

    def yz_arrive(j, carry):
        other = lax.rem(me + j, n)
        yz_copy(other, other).wait_recv()
        return carry

    lax.fori_loop(1, n, yz_arrive, 0)
    for piece in range(2):
        ring_open(piece)
    turned = yz_all[:, : 2 * HEAD_DIM].T
    k_low[...] = turned
    k_top[:HEAD_DIM] = jnp.zeros_like(turned[:HEAD_DIM])
    k_top[HEAD_DIM:] = turned[:HEAD_DIM]
    z_low[...] = jnp.concatenate(
        (
            jnp.zeros((n * rows, HEAD_DIM), BF16),
            yz_all[:, 2 * HEAD_DIM : 3 * HEAD_DIM],
        ),
        axis=1,
    )
    per = 4
    blocks = n // per
    for i in range(blocks):
        block = lax.rem(me // per + i, blocks)
        for u in range(per):
            other = block * per + u

            @pl.when(other != me)
            def _():
                x_copy(other, other).wait_recv()

        span = pl.ds(pl.multiple_of(block * per * rows, per * rows), per * rows)
        x = x_all[span]
        scores = dot(x, k_top[...])
        drift = dot(x, k_low[...])
        weights = jnp.exp(scores - jnp.max(scores, axis=1, keepdims=True))
        weights = weights * (1.0 / jnp.sum(weights, axis=1, keepdims=True))
        drifted = weights * drift
        mean = jnp.sum(drifted, axis=1, keepdims=True)
        both = dot(weights.astype(BF16), yz_all[:, 2 * HEAD_DIM :])
        low = dot(drifted.astype(BF16), z_low[...])
        attended = both[:, :HEAD_DIM]
        moved = low[:, HEAD_DIM:] - mean * attended + both[:, HEAD_DIM:]
        o_send[span] = jnp.concatenate((attended, moved), axis=1).astype(BF16)
        for u in range(per):
            other = block * per + u

            @pl.when(other != me)
            def _():
                o_copy(other, me).start()

    o_all[me] = o_send[part(me)]
    ring_step(0, 1)
    ring_step(1, 1)

    def o_arrive(j, carry):
        other = lax.rem(me + j, n)
        o_copy(other, other).wait_recv()
        return carry

    lax.fori_loop(1, n, o_arrive, 0)
    ring_step(0, 2)
    ring_step(1, 2)
    ring_open(2)
    ring_open(3)
    for h in range(0, n, 2):
        cols = slice(h * HEAD_DIM, (h + 2) * HEAD_DIM)
        one = o_all[h].astype(F32)
        two = o_all[h + 1].astype(F32)
        state[:, cols] = fetched[6, :, cols].astype(F32) + jnp.concatenate(
            (one[:, :HEAD_DIM], two[:, :HEAD_DIM]), axis=1
        )
        tangent[:, cols] = fetched[7, :, cols].astype(F32) + jnp.concatenate(
            (one[:, HEAD_DIM:], two[:, HEAD_DIM:]), axis=1
        )
    wide_state = state[...]
    wide_tangent = tangent[...]
    inverse = lax.rsqrt(jnp.mean(wide_state * wide_state, axis=1, keepdims=True) + epsilon)
    cross = jnp.mean(wide_state * wide_tangent, axis=1, keepdims=True)
    normed = (gain[...] * wide_state * inverse).astype(BF16)
    normed_tangent = (
        gain[...] * inverse * (wide_tangent - wide_state * cross * inverse * inverse)
    ).astype(BF16)
    for c in range(chunks):
        cols = slice(c * CHUNK, (c + 1) * CHUNK)
        tokens[2 * c * rows : (2 * c + 1) * rows] = normed[:, cols]
        tokens[(2 * c + 1) * rows : (2 * c + 2) * rows] = normed_tangent[:, cols]

    def m_copy(dest, slot):
        return pltpu.make_async_remote_copy(
            src_ref=message.at[dest],
            dst_ref=middle.at[slot],
            send_sem=m_sent.at[dest],
            recv_sem=m_came.at[slot],
            device_id=at_y(dest),
            device_id_type=MESH,
        )

    def f_copy(dest, source_x, source_y):
        pair = pl.ds(pl.multiple_of((dest // 2) * depth, depth), depth)
        return pltpu.make_async_remote_copy(
            src_ref=middle.at[source_y, pair],
            dst_ref=landed.at[source_x, source_y],
            send_sem=f_sent.at[dest, source_y],
            recv_sem=f_came.at[source_x, source_y],
            device_id=at_x(dest),
            device_id_type=MESH,
        )

    def fill(dest):
        picked = pick[pl.ds(pl.multiple_of(dest * 2 * depth, 2 * depth), 2 * depth)]
        return dot(picked, tokens[...]).astype(BF16)

    def spread(source_y):
        for j in (1, 3, 2):
            f_copy(lax.rem(my_x + j, X_SIZE), my_x, source_y).start()
        landed[my_x, source_y] = middle[
            source_y, pl.ds(pl.multiple_of((my_x // 2) * depth, depth), depth)
        ]

    for j in order:
        dest = lax.rem(my_y + j, y_size)
        message[dest] = fill(dest)
        m_copy(dest, my_y).start()
    middle[my_y] = fill(my_y)
    spread(my_y)
    for i, j in enumerate(order):
        other = lax.rem(my_y + j, y_size)
        m_copy(other, other).wait_recv()
        spread(other)
        if i in (1, 4):
            for piece in range(2):
                ring_step(piece, 3 if i == 1 else 4)
        if i == 5:
            ring_step(2, 1)
            ring_step(3, 1)
            ring_open(4)
            ring_open(5)
    for j in [0] + order:
        other = lax.rem(my_y + j, y_size)
        for i in range(1, X_SIZE):
            source = lax.rem(my_x + i, X_SIZE)
            f_copy(source, source, other).wait_recv()
    group = half * capacity
    for x in range(X_SIZE):
        sorted_rows = [
            dot(sort[...], landed[x, side * half : (side + 1) * half].reshape(size, CHUNK))
            for side in range(2)
        ]
        for c in range(chunks):
            for kind in range(2):
                top = (2 * c + kind) * group
                expert_rows[
                    pl.ds((kind * X_SIZE + x) * 2 * group, 2 * group),
                    pl.ds(c * CHUNK, CHUNK),
                ] = jnp.concatenate(
                    [values[top : top + group] for values in sorted_rows], axis=0
                ).astype(BF16)
    ring_step(2, 2)
    ring_step(3, 2)

    count = X_SIZE * y_size * capacity

    def project(j, carry):
        z = lax.rem(my_z + j, shards)
        for piece in range(2):
            share_copy(piece, z, 1 - core).wait_recv()
        weights = jnp.concatenate((first[2 * z], first[2 * z + 1]), axis=1)
        hidden = dot(expert_rows[...], weights)
        values, slopes = gelu_pair(hidden[:count], hidden[count:])
        cols = pl.ds(pl.multiple_of(z * 2 * units, 2 * units), 2 * units)
        active[:count, cols] = values.astype(BF16)
        active[count:, cols] = slopes.astype(BF16)
        return carry

    lax.fori_loop(0, shards, project, 0)
    block = y_size * capacity

    def h_copy(c, dest, slot):
        return pltpu.make_async_remote_copy(
            src_ref=halves_send.at[c, dest],
            dst_ref=halves.at[c, slot],
            send_sem=h_sent.at[c, dest],
            recv_sem=h_came.at[c, slot],
            device_id=at_x(dest),
            device_id_type=MESH,
        )

    def s_copy(c, dest, slot):
        return pltpu.make_async_remote_copy(
            src_ref=sums_send.at[c, dest],
            dst_ref=sums.at[c, slot],
            send_sem=s_sent.at[c, dest],
            recv_sem=s_came.at[c, slot],
            device_id=at_y(dest),
            device_id_type=MESH,
        )

    def expert_block(c):
        def arrive(z, carry):
            share_copy(2 + c, z, 1 - core).wait_recv()
            return carry

        lax.fori_loop(0, shards, arrive, 0)
        done = dot(active[...], second[:, c * CHUNK : (c + 1) * CHUNK]).astype(BF16)
        for x in range(X_SIZE):
            halves_send[c, x, :block] = done[x * block : (x + 1) * block]
            halves_send[c, x, block:] = done[count + x * block : count + (x + 1) * block]
        for j in (1, 3, 2):
            h_copy(c, lax.rem(my_x + j, X_SIZE), my_x).start()
        halves[c, my_x] = halves_send[c, my_x]

    def return_block(c):
        for j in (1, 3, 2):
            source = lax.rem(my_x + j, X_SIZE)
            h_copy(c, source, source).wait_recv()
        pair = [
            (halves[c, 2 * p].astype(F32) + halves[c, 2 * p + 1].astype(F32)).astype(BF16)
            for p in range(2)
        ]
        stacked = jnp.concatenate(
            [
                jnp.concatenate([total[:, i * 128 : (i + 1) * 128] for total in pair], axis=1)
                for i in range(parts)
            ],
            axis=0,
        )
        ready = dot(back_sort[...], stacked)
        for y in range(y_size):
            piece = ready[y * back_depth : (y + 1) * back_depth]
            sums_send[c, y] = jnp.concatenate((piece[:, :128], piece[:, 128:]), axis=0).astype(
                BF16
            )
        for j in order:
            s_copy(c, lax.rem(my_y + j, y_size), my_y).start()
        sums[c, my_y] = sums_send[c, my_y]

    def mix_block(c):
        for j in order:
            source = lax.rem(my_y + j, y_size)
            s_copy(c, source, source).wait_recv()
        values = sums[c].reshape(experts * back_depth, 128)
        mixed = (dot(gate_high[...], values) * 256.0 + dot(gate_low[...], values)) * (
            1.0 / 65536.0
        )
        for i in range(parts):
            cols = slice(c * CHUNK + i * 128, c * CHUNK + (i + 1) * 128)
            top = 2 * i * rows
            out[:, cols] = (state[:, cols] + mixed[top : top + rows]).astype(BF16)
            out_tangent[:, cols] = (
                tangent[:, cols] + mixed[top + rows : top + 2 * rows]
            ).astype(BF16)

    ring_step(2, 3)
    ring_step(3, 3)
    ring_step(4, 1)
    ring_step(5, 1)
    ring_step(2, 4)
    expert_block(0)
    ring_step(3, 4)
    ring_step(4, 2)
    ring_step(5, 2)
    expert_block(1)
    return_block(0)
    for hop in (3, 4):
        ring_step(4, hop)
        ring_step(5, hop)
    expert_block(2)
    return_block(1)
    expert_block(3)
    return_block(2)
    mix_block(0)
    return_block(3)
    for c in range(1, chunks):
        mix_block(c)

    def drain(j, carry):
        other = lax.rem(me + j, n)
        yz_copy(other, me).wait_send()
        x_copy(other, me).wait_send()
        o_copy(other, me).wait_send()
        return carry

    lax.fori_loop(1, n, drain, 0)

    def drain_shares(z, carry):
        for piece in range(RING_PIECES):
            share_copy(piece, z, core).wait_send()
        return carry

    lax.fori_loop(0, shards, drain_shares, 0)
    for piece in range(RING_PIECES):
        for way in range(2):
            for hop in range(1, hops(piece, way) + 1):
                ring_copy(piece, way, hop, False).wait_send()
    for j in order:
        m_copy(lax.rem(my_y + j, y_size), my_y).wait_send()
    for y in range(y_size):
        for j in range(1, X_SIZE):
            f_copy(lax.rem(my_x + j, X_SIZE), my_x, y).wait_send()
    for c in range(chunks):
        for j in range(1, X_SIZE):
            h_copy(c, lax.rem(my_x + j, X_SIZE), my_x).wait_send()
        for j in order:
            s_copy(c, lax.rem(my_y + j, y_size), my_y).wait_send()


def per_device(
    query_rows,
    key_rows,
    value_rows,
    query_tangent,
    key_tangent,
    value_tangent,
    stream,
    stream_tangent,
    norm_gain,
    expert_ids,
    gate_units,
    slot_index,
    weight_in,
    weight_out,
):
    n = lax.axis_size("seq")
    y_size = lax.axis_size("exp") // X_SIZE
    experts = 2 * y_size
    rows, width = stream.shape
    units = weight_out.shape[0]
    capacity = 2 * ((5 * rows + 4 * experts - 1) // (4 * experts))
    total = n * rows
    chunks = width // CHUNK
    depth = 2 * capacity * chunks
    parts = CHUNK // 128
    back_depth = parts * 2 * capacity
    block = y_size * capacity
    back_size = parts * 2 * block
    pair = 2 * HEAD_DIM
    vmem = pl.BlockSpec(memory_space=pltpu.VMEM)
    away = pl.BlockSpec(memory_space=pltpu.HBM)
    dma = pltpu.SemaphoreType.DMA

    def held(*shape):
        return pltpu.VMEM(shape, BF16)

    return pl.pallas_call(
        functools.partial(block_kernel, n, y_size, capacity),
        out_shape=(
            jax.ShapeDtypeStruct((rows, width), BF16),
            jax.ShapeDtypeStruct((rows, width), BF16),
        ),
        in_specs=[away] * 14,
        out_specs=(vmem,) * 2,
        scratch_shapes=[
            held(8, rows, width),
            pltpu.VMEM((1, width), F32),
            pltpu.VMEM((3, 2, rows), jnp.int32),
            held(n, width, units),
            held(n * units, width),
            held(n, rows, pair),
            held(n, rows, 2 * pair),
            held(total, pair),
            held(total, 2 * pair),
            held(pair, total),
            held(pair, total),
            held(total, pair),
            held(total, pair),
            held(n, rows, pair),
            held(experts * depth, 2 * chunks * rows),
            held(y_size // 2 * depth, y_size // 2 * depth),
            held(2 * chunks * rows, CHUNK),
            held(y_size, 2 * depth, CHUNK),
            held(y_size, 2 * depth, CHUNK),
            held(X_SIZE, y_size, depth, CHUNK),
            pltpu.VMEM((rows, width), F32),
            pltpu.VMEM((rows, width), F32),
            held(2 * X_SIZE * block, width),
            held(2 * X_SIZE * block, n * units),
            held(back_size, back_size),
            held(2 * parts * rows, experts * back_depth),
            held(2 * parts * rows, experts * back_depth),
            held(chunks, X_SIZE, 2 * block, CHUNK),
            held(chunks, X_SIZE, 2 * block, CHUNK),
            held(chunks, y_size, 2 * back_depth, 128),
            held(chunks, y_size, 2 * back_depth, 128),
        ]
        + [dma((14,))]
        + [dma((n,))] * 6
        + [dma((y_size,))] * 2
        + [dma((X_SIZE, y_size))] * 2
        + [dma((RING_PIECES, 2 * HOPS))] * 2
        + [dma((RING_PIECES, n // 2))] * 2
        + [dma((chunks, X_SIZE))] * 2
        + [dma((chunks, y_size))] * 2,
        compiler_params=pltpu.CompilerParams(
            collective_id=0, has_side_effects=True, vmem_limit_bytes=56 * 1024 * 1024
        ),
        name="moe_block",
    )(
        query_rows,
        key_rows,
        value_rows,
        query_tangent,
        key_tangent,
        value_tangent,
        stream,
        stream_tangent,
        norm_gain.reshape(1, width),
        expert_ids.T,
        gate_units.T,
        slot_index.T,
        weight_in,
        weight_out,
    )


def solution(mesh):
    rows = P(("exp", "seq"), None)
    return jax.shard_map(
        per_device,
        mesh=mesh,
        in_specs=(rows,) * 8 + (P(),) + (rows,) * 3 + (P(None, ("exp", "seq")), rows),
        out_specs=(rows, rows),
        check_vma=False,
    )
```

time: 231 us -> 123 us (0.53); the launches traced: 227 us -> 122 us
  waiting for transfers between devices: 97.7 us -> 0 us
  Pallas kernels: 46.6 us -> 120 us
  starting transfers between devices: 29.5 us -> 0 us
  local copies, waits for them, and re-layouts: 21.9 us -> 2.26 us
  between operations: 14.3 us -> 0.65 us
  matrix products: 9.73 us -> 0 us
  other arithmetic: 7.23 us -> 0 us
    all_to_all x4 -> x0, waiting for transfers between devices: 96.2 us -> none  [the longest x1 27.1 us: per_device(): lax.all_to_all(outgoing, 'exp', split_axis=0, concat_axis=0, tiled=True)]
    pallas_call x1, Pallas kernels: 46.6 us -> 120 us  [per_device(): pl.pallas_call(functools.partial(block_kernel, n, y_size, capacity), out_...]
    all_to_all x4 -> x0, starting transfers between devices: 29.5 us -> none  [the longest x1 10.1 us: per_device(): lax.all_to_all(outgoing, 'exp', split_axis=0, concat_axis=0, tiled=True)]
    dot_general x2 -> x0, matrix products: 9.73 us -> none  [the longest x1 5.05 us: per_device(): jnp.einsum('prn,nd->prd', activated_pair, lax.all_gather(weight_out, 'seq...]
    unnamed x22 -> x4, local copies, waits for them, and re-layouts: 7.92 us -> 2.26 us
    gather x6 -> x0, local copies, waits for them, and re-layouts: 4.1 us -> none  [the longest x2 1.11 us: per_device(): expert_sums[flat_index]]
    reduce_sum x3 -> x0, other arithmetic: 3.9 us -> none  [the longest x1 1.45 us: per_device(): jnp.sum(gate_values[:, :, None] * expert_drifts[flat_index], axis=1)]
    another operation x4 -> x0, local copies, waits for them, and re-layouts: 2.86 us -> none  [the longest x1 1.21 us: per_device(): partial_out = projected_low[0].reshape(arrived.shape)]
  transfers between devices with their start and end apart: 6 -> 0, of which waited for: 4 -> 0; matrix products, arithmetic and copies ran while one was open for 8% -> 0% of each run, Pallas kernels for 21% -> 0%
where the time goes in v3:
time: 123 us; the launch traced here: 122 us
  Pallas kernels  120 us (98%)
  local copies, waits for them, and re-layouts  2.26 us (2%)
    pallas_call x1, Pallas kernels, per_device(): pl.pallas_call(functools.partial(block_kernel, n, y_size, capacity), out_...  120 us

profile of v3, /device:TPU:1, one launch (start us, length us, event | category | flops | bytes accessed | tf_op | source)
XLA Modules:
  0.0 122.5 jit_solution(17698548902971233048)
XLA Ops:
  0.6 119.6 %moe_block.1 = (bf16[64,1024]{1,0:T(8,128)(2,1)}, bf16[64,1024]{1,0:T(8,128)(2,1)}) custom-call(bf16[64,1024]{1,0:T(8,128)(2,1)} %q_in.1, bf16[64,1024]{1,0:T(8,128)(2,1)} %k_in.1, bf16[64,1024]{1,0:T(8,128)(2,1)} %v_in.1, bf16[64,1024]{1,0:T(8,128)(2,1)} %dq_in.1, bf16[64,1024]{1,0:T(8,128)(2,1)} %dk_in.1, bf16[64,1024]{1,0:T(8,128)(2,1)} %dv_in.1, ...), custom_call_target="tpu_custom_call" | custom-call | tf_op jit(solution)/shard_map/moe_block/pallas_call | solution.py:701
  120.2 0.0 copy-start
  120.2 1.6 %copy.18 = bf16[64,1024]{1,0:T(8,128)(2,1)} copy(bf16[64,1024]{1,0:T(8,128)(2,1)} %get-tuple-element.4) | data formatting | bytes 262144
  121.8 0.0 copy-done
  121.8 0.7 copy.19
Async XLA Ops:
  120.2 1.6 %copy-start = (bf16[64,1024]{1,0:T(8,128)(2,1)S(1)}, bf16[64,1024]{1,0:T(8,128)(2,1)}, u32[]{:S(2)}) copy-start(bf16[64,1024]{1,0:T(8,128)(2,1)} %get-tuple-element.5) | copy-start | bytes 393220

commit v4 on v3

--- a/solution.py
+++ b/solution.py
@@ -50,6 +50,7 @@
 CHUNK = 256
 
 
+ROUNDS = 1
 RING_PIECES = 6
 HOPS = 4
 
@@ -361,8 +362,8 @@
         return carry
 
     lax.fori_loop(1, n, yz_arrive, 0)
-    for piece in range(2):
-        ring_open(piece)
+    ring_open(0)
+    ring_open(1)
     turned = yz_all[:, : 2 * HEAD_DIM].T
     k_low[...] = turned
     k_top[:HEAD_DIM] = jnp.zeros_like(turned[:HEAD_DIM])
@@ -408,6 +409,8 @@
     o_all[me] = o_send[part(me)]
     ring_step(0, 1)
     ring_step(1, 1)
+    ring_open(2)
+    ring_open(3)
 
     def o_arrive(j, carry):
         other = lax.rem(me + j, n)
@@ -415,10 +418,6 @@
         return carry
 
     lax.fori_loop(1, n, o_arrive, 0)
-    ring_step(0, 2)
-    ring_step(1, 2)
-    ring_open(2)
-    ring_open(3)
     for h in range(0, n, 2):
         cols = slice(h * HEAD_DIM, (h + 2) * HEAD_DIM)
         one = o_all[h].astype(F32)
@@ -442,23 +441,26 @@
         tokens[2 * c * rows : (2 * c + 1) * rows] = normed[:, cols]
         tokens[(2 * c + 1) * rows : (2 * c + 2) * rows] = normed_tangent[:, cols]
 
-    def m_copy(dest, slot):
-        return pltpu.make_async_remote_copy(
-            src_ref=message.at[dest],
-            dst_ref=middle.at[slot],
-            send_sem=m_sent.at[dest],
-            recv_sem=m_came.at[slot],
+    def round_cols(turn):
+        return slice(turn * (CHUNK // ROUNDS), (turn + 1) * (CHUNK // ROUNDS))
+
+    def m_copy(dest, slot, turn):
+        return pltpu.make_async_remote_copy(
+            src_ref=message.at[dest, :, round_cols(turn)],
+            dst_ref=middle.at[slot, :, round_cols(turn)],
+            send_sem=m_sent.at[turn, dest],
+            recv_sem=m_came.at[turn, slot],
             device_id=at_y(dest),
             device_id_type=MESH,
         )
 
-    def f_copy(dest, source_x, source_y):
+    def f_copy(dest, source_x, source_y, turn):
         pair = pl.ds(pl.multiple_of((dest // 2) * depth, depth), depth)
         return pltpu.make_async_remote_copy(
-            src_ref=middle.at[source_y, pair],
-            dst_ref=landed.at[source_x, source_y],
-            send_sem=f_sent.at[dest, source_y],
-            recv_sem=f_came.at[source_x, source_y],
+            src_ref=middle.at[source_y, pair, round_cols(turn)],
+            dst_ref=landed.at[source_x, source_y, :, round_cols(turn)],
+            send_sem=f_sent.at[turn, dest, source_y],
+            recv_sem=f_came.at[turn, source_x, source_y],
             device_id=at_x(dest),
             device_id_type=MESH,
         )
@@ -467,36 +469,52 @@
         picked = pick[pl.ds(pl.multiple_of(dest * 2 * depth, 2 * depth), 2 * depth)]
         return dot(picked, tokens[...]).astype(BF16)
 
-    def spread(source_y):
+    def spread(source_y, turn):
         for j in (1, 3, 2):
-            f_copy(lax.rem(my_x + j, X_SIZE), my_x, source_y).start()
-        landed[my_x, source_y] = middle[
-            source_y, pl.ds(pl.multiple_of((my_x // 2) * depth, depth), depth)
-        ]
+            f_copy(lax.rem(my_x + j, X_SIZE), my_x, source_y, turn).start()
 
     for j in order:
         dest = lax.rem(my_y + j, y_size)
         message[dest] = fill(dest)
-        m_copy(dest, my_y).start()
+        m_copy(dest, my_y, 0).start()
+    for turn in range(1, ROUNDS):
+        for j in order:
+            m_copy(lax.rem(my_y + j, y_size), my_y, turn).start()
     middle[my_y] = fill(my_y)
-    spread(my_y)
-    for i, j in enumerate(order):
-        other = lax.rem(my_y + j, y_size)
-        m_copy(other, other).wait_recv()
-        spread(other)
-        if i in (1, 4):
-            for piece in range(2):
-                ring_step(piece, 3 if i == 1 else 4)
-        if i == 5:
-            ring_step(2, 1)
-            ring_step(3, 1)
-            ring_open(4)
-            ring_open(5)
+    for turn in range(ROUNDS):
+        spread(my_y, turn)
+    ring_step(0, 2)
+    ring_step(1, 2)
+    for turn in range(ROUNDS):
+        for i, j in enumerate(order):
+            other = lax.rem(my_y + j, y_size)
+            m_copy(other, other, turn).wait_recv()
+            spread(other, turn)
+            if i == 1:
+                ring_step(2, 1)
+                ring_step(3, 1)
+            if i == 3:
+                ring_step(0, 3)
+                ring_step(1, 3)
+                ring_open(4)
+                ring_open(5)
+            if i == 5:
+                ring_step(2, 2)
+                ring_step(3, 2)
+            if i == 6:
+                ring_step(0, 4)
+                ring_step(1, 4)
+                ring_step(4, 1)
+                ring_step(5, 1)
+    own_pair = pl.ds(pl.multiple_of((my_x // 2) * depth, depth), depth)
+    for y in range(y_size):
+        landed[my_x, y] = middle[y, own_pair]
     for j in [0] + order:
         other = lax.rem(my_y + j, y_size)
         for i in range(1, X_SIZE):
             source = lax.rem(my_x + i, X_SIZE)
-            f_copy(source, source, other).wait_recv()
+            for turn in range(ROUNDS):
+                f_copy(source, source, other, turn).wait_recv()
     group = half * capacity
     for x in range(X_SIZE):
         sorted_rows = [
@@ -512,8 +530,10 @@
                 ] = jnp.concatenate(
                     [values[top : top + group] for values in sorted_rows], axis=0
                 ).astype(BF16)
-    ring_step(2, 2)
-    ring_step(3, 2)
+    ring_step(2, 3)
+    ring_step(3, 3)
+    ring_step(4, 2)
+    ring_step(5, 2)
 
     count = X_SIZE * y_size * capacity
 
@@ -529,7 +549,12 @@
         active[count:, cols] = slopes.astype(BF16)
         return carry
 
-    lax.fori_loop(0, shards, project, 0)
+    lax.fori_loop(0, shards // 2, project, 0)
+    ring_step(2, 4)
+    ring_step(3, 4)
+    ring_step(4, 3)
+    ring_step(5, 3)
+    lax.fori_loop(shards // 2, shards, project, 0)
     block = y_size * capacity
 
     def h_copy(c, dest, slot):
@@ -602,25 +627,14 @@
         for i in range(parts):
             cols = slice(c * CHUNK + i * 128, c * CHUNK + (i + 1) * 128)
             top = 2 * i * rows
-            out[:, cols] = (state[:, cols] + mixed[top : top + rows]).astype(BF16)
-            out_tangent[:, cols] = (
-                tangent[:, cols] + mixed[top + rows : top + 2 * rows]
-            ).astype(BF16)
-
-    ring_step(2, 3)
-    ring_step(3, 3)
-    ring_step(4, 1)
-    ring_step(5, 1)
-    ring_step(2, 4)
+            out[:, cols] = state[:, cols] + mixed[top : top + rows]
+            out_tangent[:, cols] = tangent[:, cols] + mixed[top + rows : top + 2 * rows]
+
+    ring_step(4, 4)
     expert_block(0)
-    ring_step(3, 4)
-    ring_step(4, 2)
-    ring_step(5, 2)
     expert_block(1)
     return_block(0)
-    for hop in (3, 4):
-        ring_step(4, hop)
-        ring_step(5, hop)
+    ring_step(5, 4)
     expert_block(2)
     return_block(1)
     expert_block(3)
@@ -650,10 +664,12 @@
             for hop in range(1, hops(piece, way) + 1):
                 ring_copy(piece, way, hop, False).wait_send()
     for j in order:
-        m_copy(lax.rem(my_y + j, y_size), my_y).wait_send()
+        for turn in range(ROUNDS):
+            m_copy(lax.rem(my_y + j, y_size), my_y, turn).wait_send()
     for y in range(y_size):
         for j in range(1, X_SIZE):
-            f_copy(lax.rem(my_x + j, X_SIZE), my_x, y).wait_send()
+            for turn in range(ROUNDS):
+                f_copy(lax.rem(my_x + j, X_SIZE), my_x, y, turn).wait_send()
     for c in range(chunks):
         for j in range(1, X_SIZE):
             h_copy(c, lax.rem(my_x + j, X_SIZE), my_x).wait_send()
@@ -698,11 +714,11 @@
     def held(*shape):
         return pltpu.VMEM(shape, BF16)
 
-    return pl.pallas_call(
+    block_out, block_tangent = pl.pallas_call(
         functools.partial(block_kernel, n, y_size, capacity),
         out_shape=(
-            jax.ShapeDtypeStruct((rows, width), BF16),
-            jax.ShapeDtypeStruct((rows, width), BF16),
+            jax.ShapeDtypeStruct((rows, width), F32),
+            jax.ShapeDtypeStruct((rows, width), F32),
         ),
         in_specs=[away] * 14,
         out_specs=(vmem,) * 2,
@@ -741,8 +757,8 @@
         ]
         + [dma((14,))]
         + [dma((n,))] * 6
-        + [dma((y_size,))] * 2
-        + [dma((X_SIZE, y_size))] * 2
+        + [dma((ROUNDS, y_size))] * 2
+        + [dma((ROUNDS, X_SIZE, y_size))] * 2
         + [dma((RING_PIECES, 2 * HOPS))] * 2
         + [dma((RING_PIECES, n // 2))] * 2
         + [dma((chunks, X_SIZE))] * 2
@@ -767,6 +783,7 @@
         weight_in,
         weight_out,
     )
+    return block_out.astype(BF16), block_tangent.astype(BF16)
 
 
 def solution(mesh):

time: 123 us -> 115 us (0.935)
  Pallas kernels: 120 us -> 111 us
  other arithmetic: 0 us -> 2.33 us
  local copies, waits for them, and re-layouts: 2.26 us -> 0.01 us
    pallas_call x1, Pallas kernels: 120 us -> 111 us  [per_device(): pl.pallas_call(functools.partial(block_kernel, n, y_size, capacity), out_...]
    convert_element_type x0 -> x2, other arithmetic: none -> 2.33 us  [per_device(): return (block_out.astype(BF16), block_tangent.astype(BF16))]
    unnamed x4 -> x2, local copies, waits for them, and re-layouts: 2.26 us -> 0.01 us
where the time goes in v4:
time: 115 us; the launch traced here: 114 us
  Pallas kernels  111 us (97%)
  other arithmetic  2.33 us (2%)
    pallas_call x1, Pallas kernels, per_device(): pl.pallas_call(functools.partial(block_kernel, n, y_size, capacity), out_...  111 us
    convert_element_type x2, other arithmetic, per_device(): return (block_out.astype(BF16), block_tangent.astype(BF16))  2.33 us

profile of v4, /device:TPU:1, one launch (start us, length us, event | category | flops | bytes accessed | tf_op | source)
XLA Modules:
  0.0 113.7 jit_solution(17283535918821082940)
XLA Ops:
  0.6 110.7 %moe_block.1 = (f32[64,1024]{1,0:T(8,128)}, f32[64,1024]{1,0:T(8,128)}) custom-call(bf16[64,1024]{1,0:T(8,128)(2,1)} %q_in.1, bf16[64,1024]{1,0:T(8,128)(2,1)} %k_in.1, bf16[64,1024]{1,0:T(8,128)(2,1)} %v_in.1, bf16[64,1024]{1,0:T(8,128)(2,1)} %dq_in.1, bf16[64,1024]{1,0:T(8,128)(2,1)} %dk_in.1, bf16[64,1024]{1,0:T(8,128)(2,1)} %dv_in.1, ...), custom_call_target="tpu_custom_call" | custom-call | tf_op jit(solution)/shard_map/moe_block/pallas_call | solution.py:717
  111.4 0.0 copy-start
  111.4 1.7 %convert_element_type.6 = bf16[64,1024]{1,0:T(8,128)(2,1)} convert(f32[64,1024]{1,0:T(8,128)} %get-tuple-element.4) | non-fusion elementwise | flops 65536 | bytes 393216 | tf_op jit(solution)/shard_map/convert_element_type | solution.py:786
  113.0 0.0 copy-done
  113.0 0.7 convert_element_type.7
Async XLA Ops:
  111.4 1.7 %copy-start = (f32[64,1024]{1,0:T(8,128)S(1)}, f32[64,1024]{1,0:T(8,128)}, u32[]{:S(2)}) copy-start(f32[64,1024]{1,0:T(8,128)} %get-tuple-element.5) | copy-start | bytes 786436

commit v5 on v4

--- a/solution.py
+++ b/solution.py
@@ -73,8 +73,7 @@
     slots_in,
     first_in,
     second_in,
-    out,
-    out_tangent,
+    both_out,
     fetched,
     gain,
     numbers,
@@ -627,8 +626,10 @@
         for i in range(parts):
             cols = slice(c * CHUNK + i * 128, c * CHUNK + (i + 1) * 128)
             top = 2 * i * rows
-            out[:, cols] = state[:, cols] + mixed[top : top + rows]
-            out_tangent[:, cols] = tangent[:, cols] + mixed[top + rows : top + 2 * rows]
+            both_out[:rows, cols] = (state[:, cols] + mixed[top : top + rows]).astype(BF16)
+            both_out[rows:, cols] = (
+                tangent[:, cols] + mixed[top + rows : top + 2 * rows]
+            ).astype(BF16)
 
     ring_step(4, 4)
     expert_block(0)
@@ -714,14 +715,11 @@
     def held(*shape):
         return pltpu.VMEM(shape, BF16)
 
-    block_out, block_tangent = pl.pallas_call(
+    results = pl.pallas_call(
         functools.partial(block_kernel, n, y_size, capacity),
-        out_shape=(
-            jax.ShapeDtypeStruct((rows, width), F32),
-            jax.ShapeDtypeStruct((rows, width), F32),
-        ),
+        out_shape=jax.ShapeDtypeStruct((2 * rows, width), BF16),
         in_specs=[away] * 14,
-        out_specs=(vmem,) * 2,
+        out_specs=vmem,
         scratch_shapes=[
             held(8, rows, width),
             pltpu.VMEM((1, width), F32),
@@ -783,7 +781,7 @@
         weight_in,
         weight_out,
     )
-    return block_out.astype(BF16), block_tangent.astype(BF16)
+    return results[:rows], results[rows:]
 
 
 def solution(mesh):

time: 115 us -> 114 us (level)
  other arithmetic: 2.33 us -> 0 us
  local copies, waits for them, and re-layouts: 0.01 us -> 1.68 us
    convert_element_type x2 -> x0, other arithmetic: 2.33 us -> none  [per_device(): return (block_out.astype(BF16), block_tangent.astype(BF16))]
    slice x0 -> x1, local copies, waits for them, and re-layouts: none -> 1.68 us  [per_device(): return (results[:rows], results[rows:])]
where the time goes in v5:
time: 114 us; the launch traced here: 113 us
  Pallas kernels  111 us (97%)
  local copies, waits for them, and re-layouts  1.68 us (1%)
    pallas_call x1, Pallas kernels, per_device(): pl.pallas_call(functools.partial(block_kernel, n, y_size, capacity), out_...  111 us

profile of v5, /device:TPU:1, one launch (start us, length us, event | category | flops | bytes accessed | tf_op | source)
XLA Modules:
  0.0 113.0 jit_solution(17425041274986864382)
XLA Ops:
  0.6 110.6 %moe_block.1 = bf16[128,1024]{1,0:T(8,128)(2,1)} custom-call(bf16[64,1024]{1,0:T(8,128)(2,1)} %q_in.1, bf16[64,1024]{1,0:T(8,128)(2,1)} %k_in.1, bf16[64,1024]{1,0:T(8,128)(2,1)} %v_in.1, bf16[64,1024]{1,0:T(8,128)(2,1)} %dq_in.1, bf16[64,1024]{1,0:T(8,128)(2,1)} %dk_in.1, bf16[64,1024]{1,0:T(8,128)(2,1)} %dv_in.1, bf16[64,1024]{1,0:T(8,128)(2,1)} %stream_in.1, ...), custom_call_target="tpu_custom_call" | custom-call | tf_op jit(solution)/shard_map/moe_block/pallas_call | solution.py:718
  111.3 1.7 %fusion = (bf16[64,1024]{1,0:T(8,128)(2,1)}, bf16[64,1024]{1,0:T(8,128)(2,1)}) fusion(bf16[128,1024]{1,0:T(8,128)(2,1)} %moe_block.1), kind=kLoop, calls=%fused_computation | loop fusion | bytes 524288 | tf_op jit(solution)/shard_map/slice | solution.py:784
